TPU v7x, 512 devices: a whole 4x4x16 slice. The times are simulated.
512 devices in a mesh: row: 16 (over y_lo, x, core), col: 32 (over z, y_hi).
Axes of the slice: x: 4, y: 4 (y_hi: 2, y_lo: 2; y = y_hi * 2 + y_lo), z: 16, core: 2. Of those that a mesh axis runs over, the one named last changes fastest.
Arguments:
- tokens: bfloat16 [1024, 98304], P('row', 'col'), may hold values from -6 to 6
- labels: int32 [1024, 512], P('row', 'col'), may hold values from 0 to 2
- gain_one: float32 [192], replicated, may hold values from 0.1 to 1.9
- qkv_weight: bfloat16 [192, 576], replicated, may hold values from -0.4375 to 0.4375
- proj_weight: bfloat16 [192, 192], replicated, may hold values from -0.4375 to 0.4375
- position_table: float32 [6, 225], replicated, may hold values from -4 to 300
- gain_two: float32 [192], replicated, may hold values from 0.1 to 1.9
- up_weight: bfloat16 [192, 768], replicated, may hold values from -0.4375 to 0.4375
- down_weight: bfloat16 [768, 192], replicated, may hold values from -0.21875 to 0.21875
Outputs:
- block_out: bfloat16 [1024, 98304], P('row', 'col')
All inputs are finite; a program needn't handle non-finite values.
Results may differ from a plain program's by a relative error of at most 0.006.
Values may be sent and summed in bfloat16 or wider, within the bound.
A program may use at most 64 MiB of HBM per device.

v0:
```python
import jax
import jax.numpy as jnp
import numpy as np
from jax import lax
from jax.sharding import PartitionSpec as P

C = 192
HEADS = 6
WIN = 8
HD = 32
SHIFT = 4


def shifted(block, axis, distance):
    devices = range(lax.axis_size(axis))
    route = [((i - distance) % len(devices), i) for i in devices]
    return lax.ppermute(block, axis, route)


def layer_norm(values, gain):
    values = values.astype(jnp.float32)
    mean = jnp.mean(values, axis=-1, keepdims=True)
    centred = values - mean
    variance = jnp.mean(centred * centred, axis=-1, keepdims=True)
    return centred * lax.rsqrt(variance + 1e-05) * gain


def relative_bias(position_table):
    side = np.arange(WIN)
    ys = np.repeat(side, WIN)
    xs = np.tile(side, WIN)
    where = (ys[:, None] - ys[None, :] + WIN - 1) * (2 * WIN - 1) + (
        xs[:, None] - xs[None, :] + WIN - 1
    )
    span = (2 * WIN - 1) * (2 * WIN - 1)
    selector = (np.arange(span)[:, None] == where.reshape(1, -1)).astype(np.float32)
    picked = jnp.dot(position_table, jnp.asarray(selector), precision=lax.Precision.HIGHEST)
    return picked.reshape(HEADS, WIN * WIN, WIN * WIN)


def to_windows(grid):
    nrows, ncols = (grid.shape[0], grid.shape[1])
    rest = grid.shape[2:]
    blocks = grid.reshape((nrows // WIN, WIN, ncols // WIN, WIN) + rest)
    blocks = jnp.swapaxes(blocks, 1, 2)
    return blocks.reshape((nrows // WIN * (ncols // WIN), WIN * WIN) + rest)


def from_windows(windows, nrows, ncols):
    rest = windows.shape[2:]
    blocks = windows.reshape((nrows // WIN, ncols // WIN, WIN, WIN) + rest)
    blocks = jnp.swapaxes(blocks, 1, 2)
    return blocks.reshape((nrows, ncols) + rest)


def attend(normed, group, pair_bias, qkv_weight, proj_weight):
    nrows, ncols = (normed.shape[0], normed.shape[1])
    flat = to_windows(normed).reshape(-1, C)
    count = flat.shape[0] // (WIN * WIN)
    qkv = jnp.dot(flat, qkv_weight, preferred_element_type=jnp.float32).astype(jnp.bfloat16)
    qkv = qkv.reshape(count, WIN * WIN, 3, HEADS, HD)
    scores = jnp.einsum(
        "wqhd,wkhd->whqk", qkv[:, :, 0], qkv[:, :, 1], preferred_element_type=jnp.float32
    )
    scores = scores * HD ** (-0.5) + pair_bias[None]
    ids = to_windows(group)
    allowed = ids[:, :, None] == ids[:, None, :]
    scores = jnp.where(allowed[:, None], scores, -jnp.inf)
    top = jnp.max(scores, axis=-1, keepdims=True)
    powers = jnp.exp(scores - top)
    probs = (powers / jnp.sum(powers, axis=-1, keepdims=True)).astype(jnp.bfloat16)
    attended = jnp.einsum(
        "whqk,wkhd->wqhd", probs, qkv[:, :, 2], preferred_element_type=jnp.float32
    ).astype(jnp.bfloat16)
    branch = jnp.dot(attended.reshape(-1, C), proj_weight, preferred_element_type=jnp.float32)
    return from_windows(branch.reshape(count, WIN * WIN, C), nrows, ncols)


def feed_forward(residual, gain_two, up_weight, down_weight):
    second = layer_norm(residual, gain_two).astype(jnp.bfloat16).reshape(-1, C)
    hidden = jax.nn.gelu(
        jnp.dot(second, up_weight, preferred_element_type=jnp.float32), approximate=False
    ).astype(jnp.bfloat16)
    mixed = jnp.dot(hidden, down_weight, preferred_element_type=jnp.float32).reshape(residual.shape)
    return (residual + mixed).astype(jnp.bfloat16)


def roll_forward(tile):
    below = shifted(tile[:SHIFT], "row", -1)
    extended = jnp.concatenate([tile[SHIFT:], below], axis=0)
    beside = shifted(extended[:, : SHIFT * C], "col", -1)
    return jnp.concatenate([extended[:, SHIFT * C :], beside], axis=1)


def branch_back(tile):
    above = shifted(tile[-SHIFT:].astype(jnp.bfloat16), "row", 1).astype(jnp.float32)
    extended = jnp.concatenate([above, tile[:-SHIFT]], axis=0)
    leftward = shifted(extended[:, -SHIFT * C :].astype(jnp.bfloat16), "col", 1).astype(jnp.float32)
    return jnp.concatenate([leftward, extended[:, : -SHIFT * C]], axis=1)


def local(
    tokens,
    labels,
    gain_one,
    qkv_weight,
    proj_weight,
    position_table,
    gain_two,
    up_weight,
    down_weight,
):
    nrows = tokens.shape[0]
    ncols = tokens.shape[1] // C
    row_start = lax.axis_index("row") * nrows
    col_start = lax.axis_index("col") * ncols
    row_flag = (
        row_start + jnp.arange(nrows, dtype=jnp.int32) >= nrows * lax.axis_size("row") - SHIFT
    ).astype(jnp.int32)
    col_flag = (
        col_start + jnp.arange(ncols, dtype=jnp.int32) >= ncols * lax.axis_size("col") - SHIFT
    ).astype(jnp.int32)
    group = labels * 4 + row_flag[:, None] * 2 + col_flag[None, :]
    pair_bias = relative_bias(position_table)
    moving = (
        layer_norm(tokens.reshape(nrows, ncols, C), gain_one)
        .astype(jnp.bfloat16)
        .reshape(nrows, ncols * C)
    )
    rolled = roll_forward(moving)
    normed = rolled.reshape(nrows, ncols, C)
    branch = attend(normed, group, pair_bias, qkv_weight, proj_weight)
    returned = branch_back(branch.reshape(nrows, ncols * C))
    residual = tokens.astype(jnp.float32).reshape(nrows, ncols, C) + returned.reshape(
        nrows, ncols, C
    )
    return feed_forward(residual, gain_two, up_weight, down_weight).reshape(nrows, ncols * C)


def solution(mesh):
    placed = (P("row", "col"), P("row", "col"), P(), P(), P(), P(), P(), P(), P())
    return jax.shard_map(
        local, mesh=mesh, in_specs=placed, out_specs=P("row", "col"), check_vma=False
    )
```

profile of v0, /device:TPU:8, one launch (start us, length us, event | category | flops | bytes accessed | tf_op | source)
XLA Modules:
  0.0 77.5 jit_solution(11884419510243442945)
XLA Ops:
  0.0 1.5 %reshape.88 = f32[64,16,192]{2,1,0:T(8,128)S(1)} reshape(bf16[64,3072]{1,0:T(8,128)(2,1)} %param.10) | data formatting | bytes 1179648 | tf_op jit(solution)/shard_map/convert_element_type | solution.py:21
  1.6 0.2 reduce_sum.45
  1.8 0.4 multiply_reduce_fusion.1
  2.2 0.3 multiply_convert_fusion.1
  2.7 4.0 %collective-permute-start = (bf16[4,3072]{1,0:T(4,128)(2,1)S(1)}, bf16[4,3072]{1,0:T(4,128)(2,1)S(1)}, u32[]{:S(2)}, u32[]{:S(2)}) collective-permute-start(bf16[4,3072]{1,0:T(4,128)(2,1)S(1)} %slice.44), channel_id=1, source_target_pairs={{32,0},{64,32},{96,64},{128,96},{160,128},{192,160},{224,192},{256... | collective-permute-start | bytes 73736 | tf_op jit(solution)/shard_map/ppermute | solution.py:17
  7.0 4.4 %convolution_bitcast_fusion = f32[6,4096]{1,0:T(8,128)S(1)} fusion(f32[225,4096]{1,0:T(8,128)} %constant.98.clone, f32[6,225]{1,0:T(8,128)S(1)} %copy-done.4), kind=kOutput, calls=%fused_computation.2 | convolution fusion | flops 66355200 | bytes 3790104 | tf_op jit(solution)/shard_map/dot_general | solution.py:37
  11.5 0.9 %broadcast_compare_fusion = pred[16,64,64]{1,2,0:T(8,128)(4,1)} fusion(s32[16,64]{1,0:T(8,128)S(1)} %eq.19), kind=kLoop, calls=%fused_computation.56 | loop fusion | flops 65536 | bytes 69632 | tf_op jit(solution)/shard_map/eq | solution.py:67
  12.5 0.8 %copy.31 = f32[6,64,64]{1,2,0:T(8,128)} copy(f32[6,64,64]{2,1,0:T(8,128)S(1)} %add.87) | data formatting | bytes 196608 | tf_op jit(solution)/shard_map/add | solution.py:65
  13.3 0.5 slice.42
  13.8 13.4 %collective-permute-start.1 = (bf16[64,768]{1,0:T(8,128)(2,1)S(1)}, bf16[64,768]{1,0:T(8,128)(2,1)S(1)}, u32[]{:S(2)}, u32[]{:S(2)}) collective-permute-start(bf16[64,768]{1,0:T(8,128)(2,1)S(1)} %pad_maximum_fusion.2), channel_id=1, source_target_pairs={{1,0},{2,1},{3,2},{4,3},{5,4},{6,5},{7,6},{8,7},{9,8},{10,9},{11,1... | collective-permute-start | bytes 294920 | tf_op jit(solution)/shard_map/ppermute | solution.py:17
  27.3 2.2 %collective-permute-done.1 = bf16[64,768]{1,0:T(8,128)(2,1)S(1)} collective-permute-done((bf16[64,768]{1,0:T(8,128)(2,1)S(1)}, bf16[64,768]{1,0:T(8,128)(2,1)S(1)}, u32[]{:S(2)}, u32[]{:S(2)}) %collective-permute-start.1) | collective-permute-done | bytes 98336 | tf_op jit(solution)/shard_map/ppermute | solution.py:17
  29.5 0.6 reshape_reshape.10
  30.2 1.5 %convolution_convert_fusion = bf16[1024,576]{0,1:T(8,128)(2,1)} fusion(bf16[1024,192]{1,0:T(8,128)(2,1)S(1)} %bitcast.58, bf16[192,576]{1,0:T(8,128)(2,1)S(1)} %copy-done.2), kind=kOutput, calls=%fused_computation.30 | convolution fusion | flops 227082240 | bytes 1794048 | tf_op jit(solution)/shard_map/dot_general | solution.py:60
  31.7 3.2 %reshape.85 = bf16[16,64,3,6,32]{1,0,4,3,2:T(8,128)(2,1)S(1)} reshape(bf16[1024,576]{0,1:T(8,128)(2,1)} %convolution_convert_fusion) | data formatting | bytes 2359296 | tf_op jit(solution)/shard_map/reshape | solution.py:61
  34.9 1.6 %fusion.65 = (bf16[16,64,1,6,32]{1,0,4,3,2:T(8,128)(2,1)S(1)}, bf16[16,64,1,6,32]{1,0,4,3,2:T(8,128)(2,1)}, bf16[16,64,1,6,32]{1,0,4,3,2:T(8,128)(2,1)}) fusion(bf16[16,64,3,6,32]{1,0,4,3,2:T(8,128)(2,1)S(1)} %reshape.85), kind=kLoop, calls=%fused_computation.101 | loop fusion | bytes 2359296 | tf_op jit(solution)/shard_map/slice | solution.py:73
  36.5 4.7 %fusion.66 = (f32[16,6,64]{2,1,0:T(8,128)S(1)}, f32[16,6,64,64]{2,3,1,0:T(8,128)}) fusion(f32[6,64,64]{1,2,0:T(8,128)} %copy.31, pred[16,64,64]{1,2,0:T(8,128)(4,1)} %broadcast_compare_fusion, bf16[16,64,1,6,32]{1,0,4,3,2:T(8,128)(2,1)} %get-tuple-element.7, bf16[16,64,1,6,32]{1,0,4,3,2:T(8,128)(2,1)} %get-tuple-element.6), kind=kOutput, calls=%fused_computation.102 | convolution fusion | flops 27131968 | bytes 2547712 | tf_op jit(solution)/shard_map/sub | solution.py:70
  41.3 3.3 %fusion.19 = bf16[16,64,6,32]{1,3,2,0:T(8,128)(2,1)} fusion(f32[16,6,64,64]{2,3,1,0:T(8,128)} %get-tuple-element.9, f32[16,6,64]{2,1,0:T(8,128)S(1)} %get-tuple-element.8, bf16[16,64,1,6,32]{1,0,4,3,2:T(8,128)(2,1)S(1)} %get-tuple-element.5), kind=kOutput, calls=%fused_computation.34 | convolution fusion | flops 26148864 | bytes 2383872 | tf_op jit(solution)/shard_map/whqk,wkhd->wqhd/dot_general | solution.py:72
  44.6 2.2 %copy.33 = bf16[16,64,6,32]{3,2,1,0:T(8,128)(2,1)S(1)} copy(bf16[16,64,6,32]{1,3,2,0:T(8,128)(2,1)} %fusion.19) | data formatting | bytes 786432 | tf_op jit(solution)/shard_map/convert_element_type | solution.py:74
  46.8 1.3 %dot_general.27 = bf16[8,2,8,8,192]{4,3,2,1,0:T(8,128)(2,1)S(1)} reshape(bf16[16,64,6,32]{3,2,1,0:T(8,128)(2,1)S(1)} %copy.33) | data formatting | bytes 786432 | tf_op jit(solution)/shard_map/dot_general | solution.py:75
  48.0 0.3 convolution_bitcast_fusion.1
  48.5 0.4 reshape_reshape.12
  48.9 1.9 %collective-permute-start.2 = (bf16[4,3072]{1,0:T(4,128)(2,1)S(1)}, bf16[4,3072]{1,0:T(4,128)(2,1)S(1)}, u32[]{:S(2)}, u32[]{:S(2)}) collective-permute-start(bf16[4,3072]{1,0:T(4,128)(2,1)S(1)} %slice.80), channel_id=1, source_target_pairs={{480,0},{0,32},{32,64},{64,96},{96,128},{128,160},{160,192},{192,2... | collective-permute-start | bytes 73736 | tf_op jit(solution)/shard_map/ppermute | solution.py:17
  50.8 5.3 %collective-permute-done.2 = bf16[4,3072]{1,0:T(4,128)(2,1)S(1)} collective-permute-done((bf16[4,3072]{1,0:T(4,128)(2,1)S(1)}, bf16[4,3072]{1,0:T(4,128)(2,1)S(1)}, u32[]{:S(2)}, u32[]{:S(2)}) %collective-permute-start.2) | collective-permute-done | bytes 24608 | tf_op jit(solution)/shard_map/ppermute | solution.py:17
  56.2 2.1 %collective-permute-start.3 = (bf16[64,768]{1,0:T(8,128)(2,1)S(1)}, bf16[64,768]{1,0:T(8,128)(2,1)S(1)}, u32[]{:S(2)}, u32[]{:S(2)}) collective-permute-start(bf16[64,768]{1,0:T(8,128)(2,1)S(1)} %fusion.31), channel_id=1, source_target_pairs={{31,0},{0,1},{1,2},{2,3},{3,4},{4,5},{5,6},{6,7},{7,8},{8,9},{9,10... | collective-permute-start | bytes 294920 | tf_op jit(solution)/shard_map/ppermute | solution.py:17
  58.3 8.7 %collective-permute-done.3 = bf16[64,768]{1,0:T(8,128)(2,1)S(1)} collective-permute-done((bf16[64,768]{1,0:T(8,128)(2,1)S(1)}, bf16[64,768]{1,0:T(8,128)(2,1)S(1)}, u32[]{:S(2)}, u32[]{:S(2)}) %collective-permute-start.3) | collective-permute-done | bytes 98336 | tf_op jit(solution)/shard_map/ppermute | solution.py:17
  67.1 0.5 add.92
  67.6 0.2 reduce_sum.48
  67.8 0.4 multiply_reduce_fusion
  68.3 0.5 add.91
  68.9 7.4 %fusion.18 = f32[1024,192]{1,0:T(8,128)S(1)} fusion(bf16[768,192]{0,1:T(8,128)(2,1)S(1)} %copy-done, bf16[192,768]{1,0:T(8,128)(2,1)S(1)} %copy-done.7, f32[1024,192]{1,0:T(8,128)S(1)} %add.91, f32[192]{0:T(256)S(1)} %copy-done.8, f32[1024]{0:T(1024)S(1)} %rsqrt.21, f32[1024]{0:T(1024)S(1)} %div.27), kind=kOutput, calls=%fused_computation.33 | convolution fusion | flops 655884288 | bytes 2171648 | tf_op jit(solution)/shard_map/dot_general | solution.py:84
  76.3 0.4 reshape.87
  76.7 0.8 %add_convert_fusion = bf16[64,3072]{1,0:T(8,128)(2,1)} fusion(f32[64,3072]{1,0:T(8,128)S(1)} %fusion.21, f32[64,3072]{1,0:T(8,128)S(1)} %reshape.87), kind=kLoop, calls=%fused_computation.48 | loop fusion | flops 393216 | bytes 1966080 | tf_op jit(solution)/shard_map/convert_element_type | solution.py:85
  (45 shorter events, 1.2 us)
Async XLA Ops:
  0.0 68.9 %copy-start = (bf16[768,192]{0,1:T(8,128)(2,1)S(1)}, bf16[768,192]{0,1:T(8,128)(2,1)}, u32[]{:S(2)}) copy-start(bf16[768,192]{0,1:T(8,128)(2,1)} %param.18) | copy-start | bytes 884740
  0.0 2.2 %copy-start.6 = (f32[192]{0:T(256)S(1)}, f32[192]{0:T(256)}, u32[]{:S(2)}) copy-start(f32[192]{0:T(256)} %param.12) | copy-start | bytes 2308
  0.0 6.7 %copy-start.5 = (s32[64,16]{0,1:T(8,128)S(1)}, s32[64,16]{0,1:T(8,128)}, u32[]{:S(2)}) copy-start(s32[64,16]{0,1:T(8,128)} %param.11) | copy-start | bytes 12292
  0.0 7.0 %copy-start.4 = (f32[6,225]{1,0:T(8,128)S(1)}, f32[6,225]{1,0:T(8,128)}, u32[]{:S(2)}) copy-start(f32[6,225]{1,0:T(8,128)} %param.15) | copy-start | bytes 16204
  2.7 11.2 %collective-permute-start = (bf16[4,3072]{1,0:T(4,128)(2,1)S(1)}, bf16[4,3072]{1,0:T(4,128)(2,1)S(1)}, u32[]{:S(2)}, u32[]{:S(2)}) collective-permute-start(bf16[4,3072]{1,0:T(4,128)(2,1)S(1)} %slice.44), channel_id=1, source_target_pairs={{32,0},{64,32},{96,64},{128,96},{160,128},{192,160},{224,192},{256... | collective-permute-start | bytes 73736 | tf_op jit(solution)/shard_map/ppermute | solution.py:17
  12.3 17.8 %copy-start.2 = (bf16[192,576]{1,0:T(8,128)(2,1)S(1)}, bf16[192,576]{1,0:T(8,128)(2,1)}, u32[]{:S(2)}) copy-start(bf16[192,576]{1,0:T(8,128)(2,1)} %param.13) | copy-start | bytes 663556
  13.8 15.6 %collective-permute-start.1 = (bf16[64,768]{1,0:T(8,128)(2,1)S(1)}, bf16[64,768]{1,0:T(8,128)(2,1)S(1)}, u32[]{:S(2)}, u32[]{:S(2)}) collective-permute-start(bf16[64,768]{1,0:T(8,128)(2,1)S(1)} %pad_maximum_fusion.2), channel_id=1, source_target_pairs={{1,0},{2,1},{3,2},{4,3},{5,4},{6,5},{7,6},{8,7},{9,8},{10,9},{11,1... | collective-permute-start | bytes 294920 | tf_op jit(solution)/shard_map/ppermute | solution.py:17
  44.6 3.4 %copy-start.3 = (bf16[192,192]{1,0:T(8,128)(2,1)S(1)}, bf16[192,192]{1,0:T(8,128)(2,1)}, u32[]{:S(2)}) copy-start(bf16[192,192]{1,0:T(8,128)(2,1)} %param.14) | copy-start | bytes 221188
  48.0 19.0 %copy-start.1 = (bf16[64,3072]{1,0:T(8,128)(2,1)S(1)}, bf16[64,3072]{1,0:T(8,128)(2,1)}, u32[]{:S(2)}) copy-start(bf16[64,3072]{1,0:T(8,128)(2,1)} %param.10) | copy-start | bytes 1179652
  48.9 7.3 %collective-permute-start.2 = (bf16[4,3072]{1,0:T(4,128)(2,1)S(1)}, bf16[4,3072]{1,0:T(4,128)(2,1)S(1)}, u32[]{:S(2)}, u32[]{:S(2)}) collective-permute-start(bf16[4,3072]{1,0:T(4,128)(2,1)S(1)} %slice.80), channel_id=1, source_target_pairs={{480,0},{0,32},{32,64},{64,96},{96,128},{128,160},{160,192},{192,2... | collective-permute-start | bytes 73736 | tf_op jit(solution)/shard_map/ppermute | solution.py:17
  56.2 10.8 %collective-permute-start.3 = (bf16[64,768]{1,0:T(8,128)(2,1)S(1)}, bf16[64,768]{1,0:T(8,128)(2,1)S(1)}, u32[]{:S(2)}, u32[]{:S(2)}) collective-permute-start(bf16[64,768]{1,0:T(8,128)(2,1)S(1)} %fusion.31), channel_id=1, source_target_pairs={{31,0},{0,1},{1,2},{2,3},{3,4},{4,5},{5,6},{6,7},{7,8},{8,9},{9,10... | collective-permute-start | bytes 294920 | tf_op jit(solution)/shard_map/ppermute | solution.py:17
  67.1 1.8 %copy-start.7 = (bf16[192,768]{1,0:T(8,128)(2,1)S(1)}, bf16[192,768]{1,0:T(8,128)(2,1)}, u32[]{:S(2)}) copy-start(bf16[192,768]{1,0:T(8,128)(2,1)} %param.17) | copy-start | bytes 884740
  67.1 1.8 %copy-start.8 = (f32[192]{0:T(256)S(1)}, f32[192]{0:T(256)}, u32[]{:S(2)}) copy-start(f32[192]{0:T(256)} %param.16) | copy-start | bytes 2308
where the time goes:
time: 77.9 us; the launch traced here: 77.5 us
  matrix products  21.7 us (28%)
  starting transfers between devices  21.4 us (27%)
  waiting for transfers between devices  16.2 us (21%)
  local copies, waits for them, and re-layouts  14.3 us (18%)
  other arithmetic  3.51 us (5%)
    ppermute x4, starting transfers between devices, shifted(): return lax.ppermute(block, axis, route)  21.4 us
    ppermute x4, waiting for transfers between devices, shifted(): return lax.ppermute(block, axis, route)  16.2 us
    dot_general x1, matrix products, feed_forward(): jnp.dot(hidden, down_weight, preferred_element_type=jnp.float32)  7.4 us
    sub x1, matrix products, attend(): powers = jnp.exp(scores - top)  4.73 us
    dot_general x1, matrix products, relative_bias(): jnp.dot(position_table, jnp.asarray(selector), precision=lax.Precision.HI...  4.43 us
    dot_general x1, matrix products, attend(): jnp.einsum('whqk,wkhd->wqhd', probs, qkv[:, :, 2], preferred_element_type...  3.31 us
    reshape x1, local copies, waits for them, and re-layouts, attend(): qkv = qkv.reshape(count, WIN * WIN, 3, HEADS, HD)  3.19 us
    convert_element_type x1, local copies, waits for them, and re-layouts, attend(): attended = jnp.einsum('whqk,wkhd->wqhd', probs, qkv[:, :, 2], preferred_e...  2.16 us
  transfers between devices with their start and end apart: 4, of which 3 were waited for; matrix products, arithmetic and copies ran while one was open for 9% of the time, Pallas kernels for 0%

commit v1 on v0

v1 whole, which is shorter than its diff:
```python
import functools

import jax
import jax.numpy as jnp
from jax import lax
from jax.experimental import pallas as pl
from jax.experimental.pallas import tpu as pltpu
from jax.sharding import PartitionSpec as P

C = 192
HEADS = 6
HID = 768
WIN = 8
HD = 32
SHIFT = 4
MESH = pl.DeviceIdType.MESH
F32 = jnp.float32
BF16 = jnp.bfloat16
LOG2E = 1.4426950408889634
FAR = -1e30
NT = (((1,), (1,)), ((), ()))


def layer_norm(values, gain):
    mean = jnp.sum(values, axis=-1, keepdims=True) * (1.0 / C)
    centred = values - mean
    variance = jnp.sum(centred * centred, axis=-1, keepdims=True) * (1.0 / C)
    return centred * lax.rsqrt(variance + 1e-05) * gain


def iota(shape, axis):
    return lax.broadcasted_iota(jnp.int32, shape, axis)


def kernel(
    nrow, ncol,
    tok, lab, gain_one, qkv, proj, table, gain_two, up, down,
    out,
    tok_v, lab_v, g1_v, qkv_v, proj_v, tab_v, g2_v, up_v, down_v,
    left, right, top, bot, lt, lb, rt, rb, llab, tlab, ltlab,
    ext, branch, wt, wk, gath, bias, bias_l, bias_r,
    in_sem, send_sem, recv_sem,
):
    row, col = lax.axis_index("row"), lax.axis_index("col")

    def at(dr, dc):
        return (lax.rem(row + dr + nrow, nrow), lax.rem(col + dc + ncol, ncol))

    around = [(0, 1), (1, 1), (-1, 1), (0, -1), (1, -1), (-1, -1), (1, 0), (-1, 0)]
    barrier = pltpu.get_barrier_semaphore()
    for dr, dc in around:
        pl.semaphore_signal(barrier, inc=1, device_id=at(dr, dc), device_id_type=MESH)
    loads = [
        pltpu.make_async_copy(src, dst, in_sem.at[i])
        for i, (src, dst) in enumerate([
            (tok, tok_v), (lab, lab_v), (gain_one, g1_v), (qkv, qkv_v), (proj, proj_v),
            (table, tab_v), (gain_two, g2_v), (up, up_v), (down, down_v),
        ])
    ]
    for load in loads:
        load.start()
    pl.semaphore_wait(barrier, len(around))

    first, last = pl.ds(0, 16), pl.ds(48, 16)
    west, east = pl.ds(0, 4 * C), pl.ds(12 * C, 4 * C)
    whole = pl.ds(0, 64)
    moves = [
        (tok.at[whole, east], left, (0, 1)),
        (tok.at[last, east], lt, (1, 1)),
        (tok.at[first, east], lb, (-1, 1)),
        (lab, llab, (0, 1)),
        (lab.at[pl.ds(56, 8)], ltlab, (1, 1)),
        (tok.at[whole, west], right, (0, -1)),
        (tok.at[last, west], rt, (1, -1)),
        (tok.at[first, west], rb, (-1, -1)),
        (tok.at[last], top, (1, 0)),
        (tok.at[first], bot, (-1, 0)),
        (lab.at[pl.ds(56, 8)], tlab, (1, 0)),
    ]
    copies = [
        pltpu.make_async_remote_copy(
            src_ref=src, dst_ref=dst, send_sem=send_sem.at[i], recv_sem=recv_sem.at[i],
            device_id=at(*where), device_id_type=MESH,
        )
        for i, (src, dst, where) in enumerate(moves)
    ]
    for copy in copies:
        copy.start()
    for load in loads:
        load.wait()

    eye = (iota((16, 64), 0) == iota((16, 64), 1)).astype(F32)
    apart = jnp.where(iota((64, 64), 0) < 16, (iota((64, 64), 0) != iota((64, 64), 1)).astype(F32) * FAR, 0.0)
    weights = qkv_v[...].astype(F32)
    pad = jnp.zeros((C, 64), F32)
    wt[0:C] = jnp.concatenate([weights[:, 0:C].T, pad], axis=1).astype(BF16)
    wt[C : C + 16] = jnp.concatenate([jnp.zeros((16, C), F32), eye], axis=1).astype(BF16)
    wt[C + 16 : 2 * C + 16] = jnp.concatenate([weights[:, 2 * C : 3 * C].T, pad], axis=1).astype(BF16)
    wk[0:C] = jnp.concatenate([weights[:, C : 2 * C], pad], axis=1).astype(BF16)
    wk[C : C + 64] = jnp.concatenate([jnp.zeros((64, C), F32), apart], axis=1).astype(BF16)

    spread = jnp.concatenate([tab_v[...] * LOG2E, jnp.zeros((HEADS, 256 - 225), F32)], axis=1)
    spread = jnp.concatenate([spread, jnp.zeros((8 - HEADS, 256), F32)], axis=0)
    rows = jnp.concatenate([spread] + [pltpu.roll(spread, 15 * y, 1) for y in range(1, WIN)], axis=0)
    lane = iota((256, 128), 1)
    select = (iota((256, 128), 0) == (lane % 8 + 7) * 15 + lane // 8).astype(F32)
    gath[...] = jnp.dot(rows, select, precision=lax.Precision.HIGHEST).reshape(8, 8, 128)
    for h in range(HEADS):
        strip = gath[:, h, :]
        for x in range(WIN):
            part = strip[:, (7 - x) * 8 : (7 - x) * 8 + 64]
            bias[x * 8 : x * 8 + 8, h * 64 : h * 64 + 64] = part
            bias_r[x * 8 : x * 8 + 8, h * 32 : h * 32 + 32] = part[:, 0:32]
            bias_l[x * 8 : x * 8 + 8, h * 32 : h * 32 + 32] = part[:, 32:64]

    gain = g1_v[...].reshape(1, C)
    gain_b = g2_v[...].reshape(1, C)

    def rim(above, below):
        above, below = above[...].astype(F32)[8:16], below[...].astype(F32)[0:8]
        return jnp.where(iota(above.shape, 0) >= 4, above, below)

    def place_rows(values, base, count):
        for j in range(count):
            ext[base + j, 4:68] = layer_norm(values[:, j * C : j * C + C], gain)

    def place_rim(values, base, count):
        for j in range(count):
            edge = layer_norm(values[:, j * C : j * C + C], gain)
            ext[base + j, 0:4] = edge[4:8]
            ext[base + j, 68:72] = edge[0:4]

    for j in range(0, 16, 2):
        place_rows(tok_v[:, j * C : j * C + 2 * C].astype(F32), j + 4, 2)

    def attend(b, x0, nx, table_ref, label_rows, lane0):
        nq = nx * 8
        edge_row = iota((72, 1), 0)
        at_end = ((edge_row < 8) & (row == 0)) | ((edge_row >= 64) & (row == nrow - 1))
        row_flag = ((edge_row % 8 >= 4) & at_end).astype(jnp.int32) * 2
        at_side = {0: col == 0, 1: None, 2: col == ncol - 1}[b]
        blocks = []
        for x in range(WIN):
            group = label_rows[:, lane0 + x : lane0 + x + 1] * 4 + row_flag
            if x >= 4 and at_side is not None:
                group = group + at_side.astype(jnp.int32)
            onehot = (iota((72, 64), 1) == group).astype(F32)
            block = jnp.concatenate([ext[8 * b + x], onehot], axis=1)
            blocks.append(block.reshape(9, 1, 8, 256))
        tokens = jnp.concatenate(blocks, axis=1).reshape(9 * 64, 256).astype(BF16)
        keys = jnp.dot(tokens, wk[...], preferred_element_type=F32).astype(BF16)
        both = lax.dot_general(wt[...], tokens, NT, preferred_element_type=F32)
        values = both[C + 16 :].astype(BF16)
        head_of_row = iota((C, HEADS * nq), 0) // HD
        own = head_of_row == iota((C, HEADS * nq), 1) // nq
        parts = []
        for a in range(9):
            q = both[0 : C + 16, a * 64 + x0 * 8 : a * 64 + x0 * 8 + nq]
            q = jnp.concatenate([q] * HEADS, axis=1)
            q = jnp.concatenate([jnp.where(own, q[0:C], 0.0), q[C:], jnp.zeros((48, HEADS * nq), F32)], axis=0)
            scores = jnp.dot(keys[a * 64 : a * 64 + 64], q.astype(BF16), preferred_element_type=F32)
            scores = scores * (HD ** (-0.5) * LOG2E) + table_ref[...]
            powers = jnp.exp2(scores - jnp.max(scores, axis=0, keepdims=True))
            total = jnp.sum(powers, axis=0, keepdims=True)
            probs = (powers * (1.0 / total)).astype(BF16)
            full = jnp.dot(values[:, a * 64 : a * 64 + 64], probs, preferred_element_type=F32)
            parts.append(jnp.concatenate(
                [full[h * HD : h * HD + HD, h * nq : h * nq + nq] for h in range(HEADS)], axis=0
            ))
        attended = jnp.concatenate(parts, axis=1).T.astype(BF16)
        mixed = jnp.dot(attended, proj_v[...], preferred_element_type=F32).reshape(9, nx, 8, C)
        for x in range(nx):
            branch[8 * b + x0 + x] = mixed[:, x].reshape(72, C)

    def finish(f):
        piece = tok_v[:, f * 768 : f * 768 + 768].astype(F32)
        residual = jnp.concatenate(
            [piece[:, j * C : j * C + C] + branch[4 * f + j + 4, 4:68] for j in range(4)], axis=0
        )
        second = layer_norm(residual, gain_b).astype(BF16)
        hidden = jnp.dot(second, up_v[...], preferred_element_type=F32)
        hidden = (hidden * (0.5 + 0.5 * lax.erf(hidden * 0.7071067811865476))).astype(BF16)
        done = residual + jnp.dot(hidden, down_v[...], preferred_element_type=F32)
        out[:, f * 768 : f * 768 + 768] = jnp.concatenate(
            [done[j * 64 : j * 64 + 64] for j in range(4)], axis=1
        ).astype(BF16)

    for i in (8, 9, 10):
        copies[i].wait_recv()
    place_rim(rim(top, bot), 4, 16)
    label_rows = jnp.concatenate([tlab[...], lab_v[...]], axis=0)
    attend(1, 0, 8, bias, label_rows, 0)
    finish(1)
    finish(2)
    for i in (5, 6, 7):
        copies[i].wait_recv()
    place_rows(right[...].astype(F32), 20, 4)
    place_rim(rim(rt, rb), 20, 4)
    attend(2, 0, 4, bias_r, label_rows, 8)
    finish(3)
    for i in range(5):
        copies[i].wait_recv()
    place_rows(left[...].astype(F32), 0, 4)
    place_rim(rim(lt, lb), 0, 4)
    attend(0, 4, 4, bias_l, jnp.concatenate([ltlab[...], llab[...]], axis=0), 8)
    finish(0)
    for copy in copies:
        copy.wait_send()


def local(nrow, ncol, *args):
    vmem = pltpu.VMEM
    scratch = [vmem(a.shape, a.dtype) for a in args]
    scratch += [vmem((64, 768), BF16)] * 2 + [vmem((16, 3072), BF16)] * 2 + [vmem((16, 768), BF16)] * 4
    scratch += [vmem((64, 16), jnp.int32), vmem((8, 16), jnp.int32), vmem((8, 16), jnp.int32)]
    scratch += [vmem((24, 72, C), F32)] * 2
    scratch += [vmem((2 * C + 16, 256), BF16), vmem((256, 256), BF16)]
    scratch += [vmem((8, 8, 128), F32), vmem((64, 384), F32), vmem((64, 192), F32), vmem((64, 192), F32)]
    scratch += [pltpu.SemaphoreType.DMA((9,)), pltpu.SemaphoreType.DMA((11,)), pltpu.SemaphoreType.DMA((11,))]
    return pl.pallas_call(
        functools.partial(kernel, nrow, ncol),
        out_shape=jax.ShapeDtypeStruct((64, 3072), BF16),
        in_specs=[pl.BlockSpec(memory_space=pl.ANY)] * len(args),
        out_specs=pl.BlockSpec(memory_space=vmem),
        scratch_shapes=scratch,
        compiler_params=pltpu.CompilerParams(
            collective_id=0, has_side_effects=True, vmem_limit_bytes=48 * 1024 * 1024
        ),
        name="window_block",
    )(*args)


def solution(mesh):
    placed = (P("row", "col"), P("row", "col"), P(), P(), P(), P(), P(), P(), P())
    return jax.shard_map(
        functools.partial(local, mesh.shape["row"], mesh.shape["col"]),
        mesh=mesh, in_specs=placed, out_specs=P("row", "col"), check_vma=False,
    )
```

time: 77.9 us -> 38.5 us (0.49)
  the two profiles are of different devices: /device:TPU:8 before, /device:TPU:1 now
where the time goes in v1:
time: 38.5 us; the launch traced here: 38.3 us
  Pallas kernels  33.6 us (87%)
  local copies, waits for them, and re-layouts  4.6 us (12%)
    pallas_call x1, Pallas kernels, local(): pl.pallas_call(functools.partial(kernel, nrow, ncol), out_shape=jax.Shape...  33.6 us
    unnamed x17, local copies, waits for them, and re-layouts  4.6 us

profile of v1, /device:TPU:1, one launch (start us, length us, event | category | flops | bytes accessed | tf_op | source)
XLA Modules:
  0.0 38.3 jit_solution(2551943763108127743)
XLA Ops:
  0.0 0.0 copy-start
  0.0 0.8 %copy.10.lab = s32[64,16]{1,0:T(8,128)S(1)} copy(s32[64,16]{0,1:T(8,128)} %param.10) | data formatting | bytes 8192 | tf_op args[1]
  0.8 0.0 copy-start.1
  0.8 0.0 copy-start.4
  0.8 0.0 copy-start.5
  0.9 0.0 copy-start.6
  0.9 1.2 %copy.11.down = bf16[768,192]{1,0:T(8,128)(2,1)S(1)} copy(bf16[768,192]{0,1:T(8,128)(2,1)} %param.17) | data formatting | bytes 589824 | tf_op args[8]
  2.0 0.0 copy-done
  2.1 0.0 copy-done.1
  2.1 0.0 copy-done.4
  2.1 0.0 copy-done.5
  2.1 0.0 copy-done.6
  2.1 0.0 copy-start.2
  2.1 0.9 %copy-done.2 = bf16[192,576]{1,0:T(8,128)(2,1)S(1)} copy-done((bf16[192,576]{1,0:T(8,128)(2,1)S(1)}, bf16[192,576]{1,0:T(8,128)(2,1)}, u32[]{:S(2)}) %copy-start.2) | copy-done | bytes 221208
  3.0 0.0 copy-start.3
  3.0 0.9 %copy-done.3 = bf16[192,192]{1,0:T(8,128)(2,1)S(1)} copy-done((bf16[192,192]{1,0:T(8,128)(2,1)S(1)}, bf16[192,192]{1,0:T(8,128)(2,1)}, u32[]{:S(2)}) %copy-start.3) | copy-done | bytes 73752
  3.9 33.6 %window_block.1 = bf16[64,3072]{1,0:T(8,128)(2,1)S(1)} custom-call(bf16[64,3072]{1,0:T(8,128)(2,1)S(1)} %copy-done, s32[64,16]{1,0:T(8,128)S(1)} %copy.10.lab, f32[192]{0:T(256)S(1)} %copy-done.5, bf16[192,576]{1,0:T(8,128)(2,1)S(1)} %copy-done.2, bf16[192,192]{1,0:T(8,128)(2,1)S(1)} %copy-done.3, f32[6,225]{1,0:T(8,128)S(1)} %copy-done.4, ...), custom_call_target="tpu_custom_call" | custom-call | tf_op jit(solution)/shard_map/window_block/pallas_call | solution.py:220
  37.6 0.7 %copy.13 = bf16[64,3072]{1,0:T(8,128)(2,1)} copy(bf16[64,3072]{1,0:T(8,128)(2,1)S(1)} %window_block.1) | data formatting | bytes 786432
Async XLA Ops:
  0.0 2.0 %copy-start = (bf16[64,3072]{1,0:T(8,128)(2,1)S(1)}, bf16[64,3072]{1,0:T(8,128)(2,1)}, u32[]{:S(2)}) copy-start(bf16[64,3072]{1,0:T(8,128)(2,1)} %tok.1) | copy-start | bytes 1179652
  0.8 1.2 %copy-start.1 = (bf16[192,768]{1,0:T(8,128)(2,1)S(1)}, bf16[192,768]{1,0:T(8,128)(2,1)}, u32[]{:S(2)}) copy-start(bf16[192,768]{1,0:T(8,128)(2,1)} %up.1) | copy-start | bytes 884740
  0.8 1.2 %copy-start.4 = (f32[6,225]{1,0:T(8,128)S(1)}, f32[6,225]{1,0:T(8,128)}, u32[]{:S(2)}) copy-start(f32[6,225]{1,0:T(8,128)} %table.1) | copy-start | bytes 16204
  0.8 1.2 %copy-start.5 = (f32[192]{0:T(256)S(1)}, f32[192]{0:T(256)}, u32[]{:S(2)}) copy-start(f32[192]{0:T(256)} %gain_one.1) | copy-start | bytes 2308
  0.9 1.2 %copy-start.6 = (f32[192]{0:T(256)S(1)}, f32[192]{0:T(256)}, u32[]{:S(2)}) copy-start(f32[192]{0:T(256)} %gain_two.1) | copy-start | bytes 2308
  2.1 0.9 %copy-start.2 = (bf16[192,576]{1,0:T(8,128)(2,1)S(1)}, bf16[192,576]{1,0:T(8,128)(2,1)}, u32[]{:S(2)}) copy-start(bf16[192,576]{1,0:T(8,128)(2,1)} %qkv.1) | copy-start | bytes 663556
  3.0 0.9 %copy-start.3 = (bf16[192,192]{1,0:T(8,128)(2,1)S(1)}, bf16[192,192]{1,0:T(8,128)(2,1)}, u32[]{:S(2)}) copy-start(bf16[192,192]{1,0:T(8,128)(2,1)} %proj.1) | copy-start | bytes 221188

commit v2 on v1

v2 whole, which is shorter than its diff:
```python
import functools

import jax
import jax.numpy as jnp
from jax import lax
from jax.experimental import pallas as pl
from jax.experimental.pallas import tpu as pltpu
from jax.sharding import PartitionSpec as P

C = 192
HEADS = 6
HID = 768
WIN = 8
HD = 32
MESH = pl.DeviceIdType.MESH
F32 = jnp.float32
BF16 = jnp.bfloat16
LOG2E = 1.4426950408889634
FAR = -1e30
NT = (((1,), (1,)), ((), ()))
LOGIT = (
    -2.3022072315216064, -0.10483857989311218, 9.559292084304616e-05, 0.00015938941214699298,
    -1.1452430044300854e-05, 3.8504501276293013e-07, -5.209909392789314e-09,
)


def iota(shape, axis):
    return lax.broadcasted_iota(jnp.int32, shape, axis)


def dot(a, b):
    return jnp.dot(a, b, preferred_element_type=F32)


def kernel(
    nrow, ncol,
    tok, lab, gain_one, qkv, proj, table, gain_two, up, down,
    out,
    tok_v, lab_v, g1_v, qkv_v, proj_v, tab_v, g2_v, up_v, down_v,
    left, right, top, bot, lt, lb, rt, rb, llab, tlab, ltlab,
    ext, branch, wq, wv, wk, ones, gath, bias, bias_l, bias_r, blocks64, blocks32, scores_v,
    in_sem, send_sem, recv_sem, met_sem,
):
    row, col = lax.axis_index("row"), lax.axis_index("col")
    newest, oldest = col == ncol - 1, col == 0

    def at(dr, dc):
        return (lax.rem(row + dr + nrow, nrow), lax.rem(col + dc + ncol, ncol))

    barrier = pltpu.get_barrier_semaphore()

    def greet(dr, dc):
        pl.semaphore_signal(barrier, inc=1, device_id=at(dr, dc), device_id_type=MESH)

    for dr in (0, 1, -1):
        greet(dr, -1)
        pl.when(jnp.logical_not(newest | (col == ncol - 2)))(functools.partial(greet, dr, 1))
        if dr:
            pl.when(jnp.logical_not(newest))(functools.partial(greet, dr, 0))
    loads = [
        pltpu.make_async_copy(src, dst, in_sem.at[i])
        for i, (src, dst) in enumerate([
            (tok, tok_v), (lab, lab_v), (gain_one, g1_v), (qkv, qkv_v), (proj, proj_v),
            (table, tab_v), (gain_two, g2_v), (up, up_v), (down, down_v),
        ])
    ]
    for load in loads:
        load.start()
    pl.semaphore_wait(barrier, jnp.where(newest, 3, jnp.where(oldest, 5, 8)))

    first, last, whole = pl.ds(0, 16), pl.ds(48, 16), pl.ds(0, 64)
    west, east = pl.ds(0, 4 * C), pl.ds(12 * C, 4 * C)
    moves = [
        (tok.at[whole, east], left, (0, 1)),
        (tok.at[last, east], lt, (1, 1)),
        (tok.at[first, east], lb, (-1, 1)),
        (lab, llab, (0, 1)),
        (lab, ltlab, (1, 1)),
        (tok.at[last], top, (1, 0)),
        (tok.at[first], bot, (-1, 0)),
        (lab, tlab, (1, 0)),
        (tok.at[whole, west], right, (0, -1)),
        (tok.at[last, west], rt, (1, -1)),
        (tok.at[first, west], rb, (-1, -1)),
    ]
    copies = [
        pltpu.make_async_remote_copy(
            src_ref=src, dst_ref=dst, send_sem=send_sem.at[i], recv_sem=recv_sem.at[i],
            device_id=at(*where), device_id_type=MESH,
        )
        for i, (src, dst, where) in enumerate(moves)
    ]
    EAST, ROWS, WEST = range(0, 5), range(5, 8), range(8, 11)

    def send(group):
        for i in group:
            copies[i].start()

    def arrive(group):
        for i in group:
            copies[i].wait_recv()

    def meet():
        pl.semaphore_signal(met_sem, inc=1, device_id=at(0, 1), device_id_type=MESH)

    send(EAST)
    pl.when(jnp.logical_not(newest))(functools.partial(send, ROWS))
    pl.when(jnp.logical_not(newest | oldest))(functools.partial(send, WEST))
    pl.when(col == ncol - 2)(meet)
    for load in loads:
        load.wait()

    eye = (iota((16, 64), 0) == iota((16, 64), 1)).astype(F32)
    apart = jnp.where(iota((64, 64), 0) < 16, (iota((64, 64), 0) != iota((64, 64), 1)).astype(F32) * FAR, 0.0)
    weights = qkv_v[...].astype(F32)
    pad = jnp.zeros((C, 64), F32)
    wq[0:C] = jnp.concatenate([weights[:, 0:C].T, pad], axis=1).astype(BF16)
    wq[C : C + 16] = jnp.concatenate([jnp.zeros((16, C), F32), eye], axis=1).astype(BF16)
    wv[...] = jnp.concatenate([weights[:, 2 * C : 3 * C].T, pad], axis=1).astype(BF16)
    wk[0:C] = jnp.concatenate([weights[:, C : 2 * C], pad], axis=1).astype(BF16)
    wk[C : C + 64] = jnp.concatenate([jnp.zeros((64, C), F32), apart], axis=1).astype(BF16)
    ones[...] = (iota((2 * C, 2 * C), 0) // C == iota((2 * C, 2 * C), 1) // C).astype(F32).astype(BF16)
    blocks64[...] = jnp.zeros(blocks64.shape, BF16)
    blocks32[...] = jnp.zeros(blocks32.shape, BF16)

    spread = jnp.concatenate([tab_v[...] * LOG2E, jnp.zeros((HEADS, 256 - 225), F32)], axis=1)
    spread = jnp.concatenate([spread, jnp.zeros((8 - HEADS, 256), F32)], axis=0)
    rows = jnp.concatenate([pltpu.roll(spread, 15 * ((s + 4) % 8), 1) if s != 4 else spread for s in range(WIN)], axis=0)
    lane = iota((256, 128), 1)
    select = (iota((256, 128), 0) == ((lane % 8 + 4) % 8 + 7) * 15 + lane // 8).astype(F32)
    gath[...] = jnp.dot(rows, select, precision=lax.Precision.HIGHEST).reshape(8, 8, 128)
    bias_l[...] = jnp.zeros(bias_l.shape, F32)
    bias_r[...] = jnp.zeros(bias_r.shape, F32)
    for h in range(HEADS):
        strip = gath[:, h, :]
        for x in range(WIN):
            part = strip[:, (7 - x) * 8 : (7 - x) * 8 + 64]
            bias[x * 8 : x * 8 + 8, h * 64 : h * 64 + 64] = part
            bias_r[x * 8 : x * 8 + 8, h * 32 : h * 32 + 32] = part[:, 0:32]
            bias_l[x * 8 : x * 8 + 8, h * 32 : h * 32 + 32] = part[:, 32:64]

    gain = jnp.concatenate([g1_v[...].reshape(1, C)] * 2, axis=1)
    gain_b = g2_v[...].reshape(1, C)

    def place(pieces, spots):
        tokens = jnp.concatenate(pieces, axis=0) if len(pieces) > 1 else pieces[0]
        wide = tokens.astype(F32)
        centred = wide - dot(tokens, ones[...]) * (1.0 / C)
        variance = dot((centred * centred).astype(BF16), ones[...]) * (1.0 / C)
        normed = centred * lax.rsqrt(variance + 1e-05) * gain
        size = pieces[0].shape[0]
        for i, (column, start) in enumerate(spots):
            part = normed[i * size : i * size + size]
            ext[column, start : start + size, 0:C] = part[:, 0:C]
            ext[column + 1, start : start + size, 0:C] = part[:, C:]

    def rim(above, below, base, count):
        above, below = above[...].astype(F32)[8:16], below[...].astype(F32)[0:8]
        block = jnp.where(iota(above.shape, 0) >= 4, above, below).astype(F32)
        pairs = range(count // 2)
        pieces = jnp.concatenate([block[:, 2 * C * i : 2 * C * i + 2 * C] for i in pairs], axis=0).astype(BF16)
        wide = pieces.astype(F32)
        centred = wide - dot(pieces, ones[...]) * (1.0 / C)
        variance = dot((centred * centred).astype(BF16), ones[...]) * (1.0 / C)
        normed = centred * lax.rsqrt(variance + 1e-05) * gain
        for i in pairs:
            part = normed[8 * i : 8 * i + 8]
            ext[base + 2 * i, 64:72, 0:C] = part[:, 0:C]
            ext[base + 2 * i + 1, 64:72, 0:C] = part[:, C:]

    def labels_of(above, own):
        above, own = above[...].astype(F32).T, own[...].astype(F32).T
        rows = jnp.concatenate([above[56:64], own], axis=0)
        rows = pltpu.roll(rows.reshape(9, 8, 16), 4, 1).reshape(72, 16)
        spot = iota((72, 1), 0)
        at_end = ((spot < 8) & (row == 0)) | ((spot >= 64) & (row == nrow - 1))
        return rows * 4.0 + jnp.where((spot % 8 < 4) & at_end, 2.0, 0.0)

    def attend(b, spans, x0, nx, table_ref, groups, lane0, blocks):
        nq = nx * 8
        per = 128 // nq
        wide = -(-HEADS // per)
        heads = [list(range(m * per, min(HEADS, m * per + per))) for m in range(wide)]
        count = len(spans)
        at_side = {0: oldest, 1: None, 2: newest}[b]
        lanes = iota((72, 256), 1)
        cut = []
        for x in range(WIN):
            value = ext[8 * b + x]
            turned = jnp.concatenate([value[64:72], value[0:64]], axis=0)
            value = jnp.where(iota((72, 256), 0) % 8 < 4, value, turned)
            group = groups[:, lane0 + x : lane0 + x + 1]
            if x >= 4 and at_side is not None:
                group = group + jnp.where(at_side, 1.0, 0.0)
            mark = ((lanes - C) == group.astype(jnp.int32)).astype(F32)
            cut.append(jnp.where(lanes >= C, mark, value))
        tokens = jnp.concatenate(
            [cut[x][8 * a : 8 * a + 8] for a in spans for x in range(WIN)], axis=0
        ).astype(BF16)
        asking = jnp.concatenate(
            [cut[x][8 * a : 8 * a + 8] for a in spans for x in range(x0, x0 + nx)], axis=0
        ).astype(BF16) if nx < WIN else tokens
        keys = dot(tokens, wk[...]).astype(BF16)
        queries = lax.dot_general(wq[...], asking, NT, preferred_element_type=F32)
        values = lax.dot_general(wv[...], tokens, NT, preferred_element_type=F32)

        block = iota((16, 128), 1) // nq
        block32 = iota((HD, 128), 1) // nq
        for g in range(count // per):
            some = queries[:, 128 * g : 128 * g + 128]
            turns = [some] + [pltpu.roll(some, k * nq, 1) for k in range(1, per)]
            for s in range(per):
                w = per * g + s
                code = turns[(0 - s) % per][C:]
                for t in range(1, per):
                    code = jnp.where(block == t, turns[(t - s) % per][C:], code)
                code = code.astype(BF16)
                for m in range(wide):
                    part = [
                        jnp.where(block32 == h % per, turns[(h - s) % per][h * HD : h * HD + HD], 0.0)
                        for h in heads[m]
                    ]
                    low = heads[m][0] * HD
                    blocks[w, low : low + HD * len(part), 128 * m : 128 * m + 128] = jnp.concatenate(
                        part, axis=0
                    ).astype(BF16)
                    blocks[w, C : C + 16, 128 * m : 128 * m + 128] = code
        for w in range(count):
            scores = dot(keys[w * 64 : w * 64 + 64], blocks[w])
            scores_v[w, :, 0 : 128 * wide] = scores * (HD ** (-0.5) * LOG2E) + table_ref[...]
        powers = []
        for w in range(count):
            scores = scores_v[w, :, 0 : 128 * wide]
            powers.append(jnp.exp2(scores - jnp.max(scores, axis=0, keepdims=True)).astype(BF16))
        one = jnp.ones((16, 64), BF16)
        found = []
        for w in range(count):
            mine = values[:, w * 64 : w * 64 + 64].astype(BF16)
            for m in range(wide):
                low, high = heads[m][0] * HD, heads[m][-1] * HD + HD
                sums = dot(jnp.concatenate([mine[low:high], one], axis=0), powers[w][:, 128 * m : 128 * m + 128])
                found.append(sums[0 : high - low] * (1.0 / sums[high - low : high - low + 1]))
        turned = []
        for g in range(count // per):
            rows_of = []
            for h in range(HEADS):
                m, i = h // per, h % per
                row_block = None
                for s in range(per):
                    piece = found[(per * g + s) * wide + m][i * HD : i * HD + HD]
                    if (s - h) % per:
                        piece = pltpu.roll(piece, ((s - h) % per) * nq, 1)
                    row_block = piece if s == 0 else jnp.where(block32 == s, piece, row_block)
                rows_of.append(row_block)
            turned.append(jnp.concatenate(rows_of, axis=0))
        attended = jnp.concatenate(turned, axis=1).T.astype(BF16)
        mixed = dot(attended, proj_v[...])
        for w, a in enumerate(spans):
            if a in spans[:w]:
                continue
            for x in range(nx):
                spot = w * nq + x * 8
                branch[8 * b + x0 + x - 4, 8 * a : 8 * a + 8] = mixed[spot : spot + 8]

    def finish(f):
        piece = tok_v[:, f * 768 : f * 768 + 768].astype(F32)
        upper = iota((64, C), 0) % 8 < 4
        residual = jnp.concatenate(
            [
                piece[:, j * C : j * C + C]
                + jnp.where(upper, branch[4 * f + j, 0:64], branch[4 * f + j, 8:72])
                for j in range(4)
            ],
            axis=0,
        )
        unit = ones[0:C, 0:C]
        high = residual.astype(BF16)
        low = (residual - high.astype(F32)).astype(BF16)
        centred = residual - (dot(high, unit) + dot(low, unit)) * (1.0 / C)
        variance = dot((centred * centred).astype(BF16), unit) * (1.0 / C)
        second = (centred * lax.rsqrt(variance + 1e-05) * gain_b).astype(BF16)
        hidden = dot(second, up_v[...])
        square = hidden * hidden
        logit = LOGIT[6] * square + LOGIT[5]
        for k in range(4, -1, -1):
            logit = logit * square + LOGIT[k]
        hidden = (hidden * (1.0 / (1.0 + jnp.exp2(hidden * logit)))).astype(BF16)
        done = residual + lax.dot_general(hidden, down_v[...], NT, preferred_element_type=F32)
        out[:, f * 768 : f * 768 + 768] = jnp.concatenate(
            [done[j * 64 : j * 64 + 64] for j in range(4)], axis=1
        ).astype(BF16)

    place([tok_v[:, 2 * C * i : 2 * C * i + 2 * C] for i in range(8)], [(4 + 2 * i, 0) for i in range(8)])

    @pl.when(newest)
    def _():
        pl.semaphore_wait(met_sem, 1)
        send(ROWS)
        send(WEST)

    arrive(ROWS)
    groups = labels_of(tlab, lab_v)
    rim(top, bot, 4, 16)
    attend(1, list(range(9)) + [8], 0, 8, bias, groups, 0, blocks64)
    finish(1)
    finish(2)

    @pl.when(jnp.logical_not(oldest))
    def _():
        arrive(WEST)
        place([right[:, 2 * C * i : 2 * C * i + 2 * C] for i in range(2)], [(20 + 2 * i, 0) for i in range(2)])
        rim(rt, rb, 20, 4)

    arrive(EAST)

    @pl.when(oldest)
    def _():
        send(WEST)
        arrive(WEST)
        place([right[:, 2 * C * i : 2 * C * i + 2 * C] for i in range(2)], [(20 + 2 * i, 0) for i in range(2)])
        rim(rt, rb, 20, 4)

    attend(2, list(range(9)) + [8] * 3, 0, 4, bias_r, groups, 8, blocks32)
    finish(3)
    place([left[:, 2 * C * i : 2 * C * i + 2 * C] for i in range(2)], [(2 * i, 0) for i in range(2)])
    rim(lt, lb, 0, 4)
    attend(0, list(range(9)) + [8] * 3, 4, 4, bias_l, labels_of(ltlab, llab), 8, blocks32)
    finish(0)
    for copy in copies:
        copy.wait_send()


def local(nrow, ncol, tok, lab, gain_one, qkv, proj, table, gain_two, up, down):
    args = (tok, lab.T, gain_one, qkv, proj, table, gain_two, up, down.T)
    vmem = pltpu.VMEM
    scratch = [vmem(a.shape, a.dtype) for a in args]
    scratch += [vmem((64, 768), BF16)] * 2 + [vmem((16, 3072), BF16)] * 2 + [vmem((16, 768), BF16)] * 4
    scratch += [vmem((16, 64), jnp.int32)] * 3
    scratch += [vmem((24, 72, 256), F32), vmem((16, 72, C), F32)]
    scratch += [vmem((C + 16, 256), BF16), vmem((C, 256), BF16), vmem((256, 256), BF16), vmem((2 * C, 2 * C), BF16)]
    scratch += [vmem((8, 8, 128), F32), vmem((64, 384), F32), vmem((64, 256), F32), vmem((64, 256), F32)]
    scratch += [vmem((10, 256, 384), BF16), vmem((12, 256, 256), BF16), vmem((12, 64, 384), F32)]
    scratch += [pltpu.SemaphoreType.DMA((9,)), pltpu.SemaphoreType.DMA((11,)), pltpu.SemaphoreType.DMA((11,))]
    scratch += [pltpu.SemaphoreType.REGULAR]
    return pl.pallas_call(
        functools.partial(kernel, nrow, ncol),
        out_shape=jax.ShapeDtypeStruct((64, 3072), BF16),
        in_specs=[pl.BlockSpec(memory_space=pltpu.HBM)] * len(args),
        out_specs=pl.BlockSpec(memory_space=vmem),
        scratch_shapes=scratch,
        compiler_params=pltpu.CompilerParams(
            collective_id=0, has_side_effects=True, vmem_limit_bytes=64 * 1024 * 1024
        ),
        name="window_block",
    )(*args)


def solution(mesh):
    placed = (P("row", "col"), P("row", "col"), P(), P(), P(), P(), P(), P(), P())
    return jax.shard_map(
        functools.partial(local, mesh.shape["row"], mesh.shape["col"]),
        mesh=mesh, in_specs=placed, out_specs=P("row", "col"), check_vma=False,
    )
```

time: 38.5 us -> 28.6 us (0.74)
  Pallas kernels: 33.6 us -> 26.7 us
  local copies, waits for them, and re-layouts: 4.6 us -> 1.77 us
    pallas_call x1, Pallas kernels: 33.6 us -> 26.7 us  [local(): pl.pallas_call(functools.partial(kernel, nrow, ncol), out_shape=jax.Shape...]
    unnamed x17 -> x1, local copies, waits for them, and re-layouts: 4.6 us -> 1.77 us
where the time goes in v2:
time: 28.6 us; the launch traced here: 28.4 us
  Pallas kernels  26.7 us (93%)
  local copies, waits for them, and re-layouts  1.77 us (6%)
    pallas_call x1, Pallas kernels, local(): pl.pallas_call(functools.partial(kernel, nrow, ncol), out_shape=jax.Shape...  26.7 us
    unnamed x1, local copies, waits for them, and re-layouts  1.77 us

profile of v2, /device:TPU:1, one launch (start us, length us, event | category | flops | bytes accessed | tf_op | source)
XLA Modules:
  0.0 28.4 jit_solution(15510312892360443787)
XLA Ops:
  0.0 26.7 %window_block.1 = bf16[64,3072]{1,0:T(8,128)(2,1)} custom-call(bf16[64,3072]{1,0:T(8,128)(2,1)} %tok.1, s32[16,64]{1,0:T(8,128)} %bitcast.3, f32[192]{0:T(256)} %gain_one.1, bf16[192,576]{1,0:T(8,128)(2,1)} %qkv.1, bf16[192,192]{1,0:T(8,128)(2,1)} %proj.1, f32[6,225]{1,0:T(8,128)} %table.1, f32[192]{0:T(256)} %gain_two.1, bf16[192,768]{1,0:T(8,128)(2,1)} %up.1, ...), custom_call_target="tpu_custom_call" | custom-call | tf_op jit(solution)/shard_map/window_block/pallas_call | solution.py:345
  26.7 1.8 %copy.11 = bf16[64,3072]{1,0:T(8,128)(2,1)} copy(bf16[64,3072]{1,0:T(8,128)(2,1)} %window_block.1) | data formatting | bytes 786432

commit v3 on v2

v3 whole, which is shorter than its diff:
```python
import functools

import jax
import jax.numpy as jnp
from jax import lax
from jax.experimental import pallas as pl
from jax.experimental.pallas import tpu as pltpu
from jax.sharding import PartitionSpec as P

C = 192
HEADS = 6
HID = 768
WIN = 8
HD = 32
MESH = pl.DeviceIdType.MESH
F32 = jnp.float32
BF16 = jnp.bfloat16
LOG2E = 1.4426950408889634
FAR = -1e30
NT = (((1,), (1,)), ((), ()))
LOGIT = (
    -2.3022072315216064, -0.10483857989311218, 9.559292084304616e-05, 0.00015938941214699298,
    -1.1452430044300854e-05, 3.8504501276293013e-07, -5.209909392789314e-09,
)


def iota(shape, axis):
    return lax.broadcasted_iota(jnp.int32, shape, axis)


def dot(a, b):
    return jnp.dot(a, b, preferred_element_type=F32)


def kernel(
    nrow, ncol,
    tok, lab, gain_one, qkv, proj, table, gain_two, up, down,
    out,
    tok_v, lab_v, g1_v, qkv_v, proj_v, tab_v, g2_v, up_v, down_v,
    beside, corner, top, bot, llab, tlab, ltlab,
    last_all, first_all, last_east, first_east, last_west, first_west,
    ext, branch, groups, wq, wv, wk, gath, bias, bias_s, blocks64, blocks32, scores_v,
    in_sem, send_sem, recv_sem, met_sem,
):
    row, col = lax.axis_index("row"), lax.axis_index("col")
    newest, oldest = col == ncol - 1, col == 0

    def at(dr, dc):
        return (lax.rem(row + dr + nrow, nrow), lax.rem(col + dc + ncol, ncol))

    barrier = pltpu.get_barrier_semaphore()

    def greet(dr, dc):
        pl.semaphore_signal(barrier, inc=1, device_id=at(dr, dc), device_id_type=MESH)

    for dr in (0, 1, -1):
        greet(dr, -1)
        pl.when(jnp.logical_not(newest | (col == ncol - 2)))(functools.partial(greet, dr, 1))
        if dr:
            pl.when(jnp.logical_not(newest))(functools.partial(greet, dr, 0))
    loads = [
        pltpu.make_async_copy(src, dst, in_sem.at[i])
        for i, (src, dst) in enumerate([
            (tok, tok_v), (lab, lab_v), (table, tab_v), (qkv, qkv_v), (gain_one, g1_v),
            (proj, proj_v), (gain_two, g2_v), (up, up_v), (down, down_v),
        ])
    ]
    for load in loads:
        load.start()

    whole = pl.ds(0, 64)
    west, east = pl.ds(0, 4 * C), pl.ds(12 * C, 4 * C)
    moves = [
        (tok.at[whole, east], beside.at[0], (0, 1)),
        (lab, llab, (0, 1)),
        (lab, ltlab, (1, 1)),
        (last_east, corner.at[0, 0], (1, 1)),
        (first_east, corner.at[0, 1], (-1, 1)),
        (last_all, top, (1, 0)),
        (first_all, bot, (-1, 0)),
        (lab, tlab, (1, 0)),
        (tok.at[whole, west], beside.at[1], (0, -1)),
        (last_west, corner.at[1, 0], (1, -1)),
        (first_west, corner.at[1, 1], (-1, -1)),
    ]
    copies = [
        pltpu.make_async_remote_copy(
            src_ref=src, dst_ref=dst, send_sem=send_sem.at[i], recv_sem=recv_sem.at[i],
            device_id=at(*where), device_id_type=MESH,
        )
        for i, (src, dst, where) in enumerate(moves)
    ]
    EAST, ROWS, WEST = range(0, 5), range(5, 8), range(8, 11)

    def send(group):
        for i in group:
            copies[i].start()

    def arrive(group):
        for i in group:
            copies[i].wait_recv()

    def meet(dr):
        pl.semaphore_signal(met_sem, inc=1, device_id=at(dr, 1), device_id_type=MESH)

    @pl.when(newest)
    def _():
        pl.semaphore_wait(barrier, 3)
        send(EAST[:3])
        for dr in (0, 1, -1):
            meet(dr)

    loads[0].wait()

    def pack(rows, high, width, packed):
        rows = rows.astype(F32)
        turned = pltpu.roll(rows, 4, 0)
        low, high = (turned, rows) if high else (rows, turned)
        pieces = []
        for i in range(0, rows.shape[1], 2 * width):
            below = high[:, i + width : i + 2 * width]
            if below.shape[1] == 0:
                below = high[:, i : i + width]
            pieces.append(jnp.where(iota((8, width), 0) < 4, low[:, i : i + width], below))
        packed[...] = jnp.concatenate(pieces, axis=0).astype(BF16)

    foot, crown = tok_v[48:64][8:16], tok_v[0:16][0:8]
    pack(foot[:, 12 * C :], True, 256, last_east)
    pack(crown[:, 12 * C :], False, 256, first_east)

    @pl.when(newest)
    def _():
        send(EAST[3:])

    for load in loads[1:5]:
        load.wait()
    pack(foot, True, 768, last_all)
    pack(crown, False, 768, first_all)
    pack(foot[:, 0 : 4 * C], True, 256, last_west)
    pack(crown[:, 0 : 4 * C], False, 256, first_west)

    eye = (iota((16, 64), 0) == iota((16, 64), 1)).astype(F32)
    apart = jnp.where(iota((64, 64), 0) < 16, (iota((64, 64), 0) != iota((64, 64), 1)).astype(F32) * FAR, 0.0)
    weights = qkv_v[...].astype(F32)
    pad = jnp.zeros((C, 64), F32)
    wq[0:C] = jnp.concatenate([weights[:, 0:C].T, pad], axis=1).astype(BF16)
    wq[C : C + 16] = jnp.concatenate([jnp.zeros((16, C), F32), eye], axis=1).astype(BF16)
    wv[...] = jnp.concatenate([weights[:, 2 * C : 3 * C].T, pad], axis=1).astype(BF16)
    wk[0:C] = jnp.concatenate([weights[:, C : 2 * C], pad], axis=1).astype(BF16)
    wk[C : C + 64] = jnp.concatenate([jnp.zeros((64, C), F32), apart], axis=1).astype(BF16)
    blocks64[...] = jnp.zeros(blocks64.shape, BF16)
    blocks32[...] = jnp.zeros(blocks32.shape, BF16)

    spread = jnp.concatenate([tab_v[...] * LOG2E, jnp.zeros((HEADS, 256 - 225), F32)], axis=1)
    spread = jnp.concatenate([spread, jnp.zeros((8 - HEADS, 256), F32)], axis=0)
    rows = jnp.concatenate([pltpu.roll(spread, 15 * ((s + 4) % 8), 1) if s != 4 else spread for s in range(WIN)], axis=0)
    lane = iota((256, 128), 1)
    select = (iota((256, 128), 0) == ((lane % 8 + 4) % 8 + 7) * 15 + lane // 8).astype(F32)
    gath[...] = jnp.dot(rows, select, precision=lax.Precision.HIGHEST).reshape(8, 8, 128)
    bias_s[...] = jnp.zeros(bias_s.shape, F32)
    for h in range(HEADS):
        strip = gath[:, h, :]
        for x in range(WIN):
            part = strip[:, (7 - x) * 8 : (7 - x) * 8 + 64]
            other = (x + 4) % 8
            bias[x * 8 : x * 8 + 8, h * 64 : h * 64 + 64] = part
            bias_s[1, x * 8 : x * 8 + 8, h * 32 : h * 32 + 32] = part[:, 0:32]
            bias_s[0, other * 8 : other * 8 + 8, h * 32 : h * 32 + 32] = part[:, 32:64]

    gain = g1_v[...].reshape(1, C)
    unit = jnp.ones((C, 128), BF16)

    def mean(values):
        total = dot(values, unit) * (1.0 / C)
        return jnp.concatenate([total, total[:, 0 : C - 128]], axis=1)

    def place(columns, base, start):
        size = columns[0].shape[0]
        tokens = jnp.concatenate(columns, axis=0)
        centred = tokens - mean(tokens.astype(BF16))
        normed = centred * lax.rsqrt(mean((centred * centred).astype(BF16)) + 1e-05) * gain
        for j in range(len(columns)):
            ext[base + j, start : start + size, 0:C] = normed[j * size : j * size + size]

    def split(wide):
        return [wide[:, C * j : C * j + C] for j in range(wide.shape[1] // C)]

    def rim(above, below, base, count):
        above, below = above.astype(F32), below.astype(F32)
        width = above.shape[1]
        parts = []
        for i in range(count * C // width):
            t = i // 2 * 8
            over, under = above[t : t + 8], below[t : t + 8]
            over, under = (over, pltpu.roll(under, 4, 0)) if i % 2 else (pltpu.roll(over, 4, 0), under)
            parts.append(jnp.where(iota((8, width), 0) >= 4, over, under))
        place(split(jnp.concatenate(parts, axis=1)), base, 64)

    def labels_of(above, own):
        above, own = above[...].astype(F32).T, own[...].astype(F32).T
        rows = jnp.concatenate([above[56:64], own], axis=0)
        rows = pltpu.roll(rows.reshape(9, 8, 16), 4, 1).reshape(72, 16)
        spot = iota((72, 1), 0)
        at_end = ((spot < 8) & (row == 0)) | ((spot >= 64) & (row == nrow - 1))
        return rows * 4.0 + jnp.where((spot % 8 < 4) & at_end, 2.0, 0.0)

    def attend(spans, real, nx, column_of, base, table_of, marks, blocks):
        nq = nx * 8
        per = 128 // nq
        wide = -(-HEADS // per)
        heads = [list(range(m * per, min(HEADS, m * per + per))) for m in range(wide)]
        count = len(spans)
        lanes = iota((72, 256), 1)
        pieces = []
        for x in range(WIN):
            value = ext[column_of(x)]
            turned = jnp.concatenate([value[64:72], value[0:64]], axis=0)
            value = jnp.where(iota((72, 256), 0) % 8 < 4, value, turned)
            mark = ((lanes - C).astype(F32) == marks[:, x : x + 1]).astype(F32)
            pieces.append(jnp.where(lanes >= C, mark, value))
        tokens = jnp.concatenate(
            [pieces[x][8 * a : 8 * a + 8] for a in spans[:real] for x in range(WIN)], axis=0
        ).astype(BF16)
        asking = jnp.concatenate(
            [pieces[x][8 * a : 8 * a + 8] for a in spans for x in range(nx)], axis=0
        ).astype(BF16)
        keys = dot(tokens, wk[...]).astype(BF16)
        queries = lax.dot_general(wq[...], asking, NT, preferred_element_type=F32)
        values = lax.dot_general(wv[...], tokens, NT, preferred_element_type=F32)

        block = iota((16, 128), 1) // nq
        block32 = iota((HD, 128), 1) // nq
        for g in range(count // per):
            some = queries[:, 128 * g : 128 * g + 128]
            turns = [some] + [pltpu.roll(some, k * nq, 1) for k in range(1, per)]
            for s in range(min(per, real - per * g)):
                w = per * g + s
                code = turns[(0 - s) % per][C:]
                for t in range(1, per):
                    code = jnp.where(block == t, turns[(t - s) % per][C:], code)
                code = code.astype(BF16)
                for m in range(wide):
                    part = [
                        jnp.where(block32 == h % per, turns[(h - s) % per][h * HD : h * HD + HD], 0.0)
                        for h in heads[m]
                    ]
                    low = heads[m][0] * HD
                    blocks[w, low : low + HD * len(part), 128 * m : 128 * m + 128] = jnp.concatenate(
                        part, axis=0
                    ).astype(BF16)
                    blocks[w, C : C + 16, 128 * m : 128 * m + 128] = code
        table = table_of()
        for w in range(real):
            scores = dot(keys[w * 64 : w * 64 + 64], blocks[w])
            scores_v[w, :, 0 : 128 * wide] = scores * (HD ** (-0.5) * LOG2E) + table
        powers = []
        for w in range(real):
            scores = scores_v[w, :, 0 : 128 * wide]
            powers.append(jnp.exp2(scores - jnp.max(scores, axis=0, keepdims=True)).astype(BF16))
        one = jnp.ones((16, 64), BF16)
        found = []
        for w in range(real):
            mine = values[:, w * 64 : w * 64 + 64].astype(BF16)
            for m in range(wide):
                low, high = heads[m][0] * HD, heads[m][-1] * HD + HD
                sums = dot(jnp.concatenate([mine[low:high], one], axis=0), powers[w][:, 128 * m : 128 * m + 128])
                found.append(sums[0 : high - low] * (1.0 / sums[high - low : high - low + 1]))
        turned = []
        for g in range(count // per):
            rows_of = []
            for h in range(HEADS):
                m, i = h // per, h % per
                row_block = None
                for s in range(min(per, real - per * g)):
                    piece = found[(per * g + s) * wide + m][i * HD : i * HD + HD]
                    if (s - h) % per:
                        piece = pltpu.roll(piece, ((s - h) % per) * nq, 1)
                    row_block = piece if s == 0 else jnp.where(block32 == s, piece, row_block)
                rows_of.append(row_block)
            turned.append(jnp.concatenate(rows_of, axis=0))
        attended = jnp.concatenate(turned, axis=1).T.astype(BF16)
        mixed = dot(attended, proj_v[...])
        for w, a in enumerate(spans[:real]):
            for x in range(nx):
                spot = w * nq + x * 8
                branch[base + x, 8 * a : 8 * a + 8] = mixed[spot : spot + 8]

    def finish(f, size):
        lanes = pl.ds(f * 768 if isinstance(f, int) else pl.multiple_of(f * 768, 768), size * C)
        columns = split(tok_v[:, lanes].astype(F32))
        upper = iota((64, C), 0) % 8 < 4
        residual = jnp.concatenate(
            [
                columns[j] + jnp.where(upper, branch[4 * f + j, 0:64], branch[4 * f + j, 8:72])
                for j in range(size)
            ],
            axis=0,
        )
        high = residual.astype(BF16)
        low = (residual - high.astype(F32)).astype(BF16)
        centred = residual - (mean(high) + mean(low))
        variance = mean((centred * centred).astype(BF16))
        second = (centred * lax.rsqrt(variance + 1e-05) * g2_v[...].reshape(1, C)).astype(BF16)
        hidden = dot(second, up_v[...])
        square = hidden * hidden
        logit = LOGIT[6] * square + LOGIT[5]
        for k in range(4, -1, -1):
            logit = logit * square + LOGIT[k]
        hidden = (hidden * (1.0 / (1.0 + jnp.exp2(hidden * logit)))).astype(BF16)
        done = residual + lax.dot_general(hidden, down_v[...], NT, preferred_element_type=F32)
        out[:, lanes] = jnp.concatenate([done[j * 64 : j * 64 + 64] for j in range(size)], axis=1).astype(BF16)

    place(split(tok_v[...].astype(F32)), 4, 0)

    @pl.when(jnp.logical_not(newest))
    def _():
        pl.semaphore_wait(barrier, jnp.where(oldest, 5, 8))
        send(EAST)
        send(ROWS)
        pl.when(jnp.logical_not(oldest))(functools.partial(send, WEST))
        pl.when(col == ncol - 2)(functools.partial(meet, 0))

    loads[5].wait()
    attend([1, 2, 3, 4, 5, 6, 7, 7], 7, 8, lambda x: 8 + x, 4, lambda: bias[...], labels_of(lab_v, lab_v), blocks64)

    @pl.when(newest)
    def _():
        pl.semaphore_wait(met_sem, 1)
        send(ROWS)
        send(WEST)

    arrive(ROWS)
    marks = labels_of(tlab, lab_v)
    place_x = iota((72, 8), 1)
    groups[1] = marks[:, 8:16] + jnp.where((place_x >= 4) & newest, 1.0, 0.0)
    rim(top[...], bot[...], 4, 16)
    attend([0, 8], 2, 8, lambda x: 8 + x, 4, lambda: bias[...], marks, blocks64)
    for load in loads[6:]:
        load.wait()
    finish(1, 8)

    def edge(i, carry):
        side = jnp.where(newest, i, 1 - i)

        @pl.when(side == 1)
        def _():
            arrive(WEST)

        @pl.when((side == 0) & oldest)
        def _():
            pl.semaphore_wait(met_sem, 3)
            send(WEST)

        @pl.when(side == 0)
        def _():
            arrive(EAST)
            near = labels_of(ltlab, llab)
            near = jnp.concatenate([near[:, 12:16], near[:, 8:12]], axis=1)
            groups[0] = near + jnp.where((place_x < 4) & oldest, 1.0, 0.0)

        place(split(beside[side].astype(F32)), 20 * side, 0)
        rim(corner[side, 0], corner[side, 1], 20 * side, 4)
        attend(
            list(range(9)) + [8] * 3, 9, 4,
            lambda x: 16 * side + x + (1 - side) * (4 if x < 4 else -4),
            12 * side, lambda: bias_s[side], groups[side], blocks32,
        )
        finish(3 * side, 4)
        return carry

    lax.fori_loop(0, 2, edge, 0)
    for copy in copies:
        copy.wait_send()


def local(nrow, ncol, tok, lab, gain_one, qkv, proj, table, gain_two, up, down):
    args = (tok, lab.T, gain_one, qkv, proj, table, gain_two, up, down.T)
    vmem = pltpu.VMEM
    scratch = [vmem(a.shape, a.dtype) for a in args]
    args = [pltpu.with_memory_space_constraint(a, pltpu.HBM) for a in args]
    scratch += [vmem((2, 64, 768), BF16), vmem((2, 2, 16, 256), BF16)] + [vmem((16, 768), BF16)] * 2
    scratch += [vmem((16, 64), jnp.int32)] * 3
    scratch += [vmem((16, 768), BF16)] * 2 + [vmem((16, 256), BF16)] * 4
    scratch += [vmem((24, 72, 256), F32), vmem((16, 72, C), F32), vmem((2, 72, 8), F32)]
    scratch += [vmem((C + 16, 256), BF16), vmem((C, 256), BF16), vmem((256, 256), BF16)]
    scratch += [vmem((8, 8, 128), F32), vmem((64, 384), F32), vmem((2, 64, 256), F32)]
    scratch += [vmem((10, 256, 384), BF16), vmem((12, 256, 256), BF16), vmem((12, 64, 384), F32)]
    scratch += [pltpu.SemaphoreType.DMA((9,)), pltpu.SemaphoreType.DMA((11,)), pltpu.SemaphoreType.DMA((11,))]
    scratch += [pltpu.SemaphoreType.REGULAR]
    return pl.pallas_call(
        functools.partial(kernel, nrow, ncol),
        out_shape=vmem((64, 3072), BF16),
        in_specs=[pl.BlockSpec(memory_space=pltpu.HBM)] * len(args),
        out_specs=pl.BlockSpec(memory_space=vmem),
        scratch_shapes=scratch,
        compiler_params=pltpu.CompilerParams(
            collective_id=0, has_side_effects=True, vmem_limit_bytes=56 * 1024 * 1024
        ),
        name="window_block",
    )(*args)


def solution(mesh):
    placed = (P("row", "col"), P("row", "col"), P(), P(), P(), P(), P(), P(), P())
    return jax.shard_map(
        functools.partial(local, mesh.shape["row"], mesh.shape["col"]),
        mesh=mesh, in_specs=placed, out_specs=P("row", "col"), check_vma=False,
    )
```

time: 28.6 us -> 23.1 us (0.81)
  Pallas kernels: 26.7 us -> 22.2 us
  local copies, waits for them, and re-layouts: 1.77 us -> 0.75 us
    pallas_call x1, Pallas kernels: 26.7 us -> 22.2 us  [local(): pl.pallas_call(functools.partial(kernel, nrow, ncol), out_shape=vmem((64,...]
    unnamed x1, local copies, waits for them, and re-layouts: 1.77 us -> 0.75 us
where the time goes in v3:
time: 23.1 us; the launch traced here: 23 us
  Pallas kernels  22.2 us (96%)
  local copies, waits for them, and re-layouts  0.75 us (3%)
    pallas_call x1, Pallas kernels, local(): pl.pallas_call(functools.partial(kernel, nrow, ncol), out_shape=vmem((64,...  22.2 us
    unnamed x1, local copies, waits for them, and re-layouts  0.75 us

profile of v3, /device:TPU:1, one launch (start us, length us, event | category | flops | bytes accessed | tf_op | source)
XLA Modules:
  0.0 23.0 jit_solution(16259924400785880123)
XLA Ops:
  0.0 22.2 %window_block.1 = bf16[64,3072]{1,0:T(8,128)(2,1)S(1)} custom-call(bf16[64,3072]{1,0:T(8,128)(2,1)} %tok.1, s32[16,64]{1,0:T(8,128)} %bitcast.3, f32[192]{0:T(256)} %gain_one.1, bf16[192,576]{1,0:T(8,128)(2,1)} %qkv.1, bf16[192,192]{1,0:T(8,128)(2,1)} %proj.1, f32[6,225]{1,0:T(8,128)} %table.1, f32[192]{0:T(256)} %gain_two.1, bf16[192,768]{1,0:T(8,128)(2,1)} %up.1, ...), custom_call_target="tpu_custom_call" | custom-call | tf_op jit(solution)/shard_map/window_block/pallas_call | solution.py:390
  22.2 0.7 %copy.11 = bf16[64,3072]{1,0:T(8,128)(2,1)} copy(bf16[64,3072]{1,0:T(8,128)(2,1)S(1)} %window_block.1) | data formatting | bytes 786432

commit v4 on v3

--- a/solution.py
+++ b/solution.py
@@ -32,18 +32,36 @@
     return jnp.dot(a, b, preferred_element_type=F32)
 
 
+def in_pieces(step, apply, *arrays):
+    return jnp.concatenate(
+        [apply(*(a[i : i + step] for a in arrays)) for i in range(0, arrays[0].shape[0], step)], axis=0
+    )
+
+
+def gelu(v):
+    square = v * v
+    logit = LOGIT[6] * square + LOGIT[5]
+    for k in range(4, -1, -1):
+        logit = logit * square + LOGIT[k]
+    return (v * (1.0 / (1.0 + jnp.exp2(v * logit)))).astype(BF16)
+
+
 def kernel(
     nrow, ncol,
     tok, lab, gain_one, qkv, proj, table, gain_two, up, down,
     out,
     tok_v, lab_v, g1_v, qkv_v, proj_v, tab_v, g2_v, up_v, down_v,
     beside, corner, top, bot, llab, tlab, ltlab,
-    last_all, first_all, last_east, first_east, last_west, first_west,
+    last_all, first_all,
     ext, branch, groups, wq, wv, wk, gath, bias, bias_s, blocks64, blocks32, scores_v,
-    in_sem, send_sem, recv_sem, met_sem,
+    in_sem, send_sem, recv_sem, met_sem, first_sem,
 ):
     row, col = lax.axis_index("row"), lax.axis_index("col")
     newest, oldest = col == ncol - 1, col == 0
+    corner_row = (row <= 1) | (row == nrow - 1)
+    first = (row == 0) & oldest
+    near_first = corner_row & (col <= 1) & jnp.logical_not(first)
+    early = newest | first
 
     def at(dr, dc):
         return (lax.rem(row + dr + nrow, nrow), lax.rem(col + dc + ncol, ncol))
@@ -55,33 +73,22 @@
 
     for dr in (0, 1, -1):
         greet(dr, -1)
-        pl.when(jnp.logical_not(newest | (col == ncol - 2)))(functools.partial(greet, dr, 1))
-        if dr:
-            pl.when(jnp.logical_not(newest))(functools.partial(greet, dr, 0))
-    loads = [
-        pltpu.make_async_copy(src, dst, in_sem.at[i])
-        for i, (src, dst) in enumerate([
-            (tok, tok_v), (lab, lab_v), (table, tab_v), (qkv, qkv_v), (gain_one, g1_v),
-            (proj, proj_v), (gain_two, g2_v), (up, up_v), (down, down_v),
-        ])
-    ]
-    for load in loads:
-        load.start()
-
+    expected = jnp.where(newest, 3, jnp.where(oldest, 5, 8)) - near_first.astype(jnp.int32)
+    foot, crown, waist = pl.ds(48, 16), pl.ds(0, 16), pl.ds(16, 32)
     whole = pl.ds(0, 64)
     west, east = pl.ds(0, 4 * C), pl.ds(12 * C, 4 * C)
     moves = [
+        (tok.at[foot, east], corner.at[0, 0], (1, 1)),
+        (tok.at[crown, east], corner.at[0, 1], (-1, 1)),
+        (lab, ltlab, (1, 1)),
+        (lab, llab, (0, 1)),
         (tok.at[whole, east], beside.at[0], (0, 1)),
-        (lab, llab, (0, 1)),
-        (lab, ltlab, (1, 1)),
-        (last_east, corner.at[0, 0], (1, 1)),
-        (first_east, corner.at[0, 1], (-1, 1)),
         (last_all, top, (1, 0)),
         (first_all, bot, (-1, 0)),
         (lab, tlab, (1, 0)),
+        (tok.at[foot, west], corner.at[1, 0], (1, -1)),
+        (tok.at[crown, west], corner.at[1, 1], (-1, -1)),
         (tok.at[whole, west], beside.at[1], (0, -1)),
-        (last_west, corner.at[1, 0], (1, -1)),
-        (first_west, corner.at[1, 1], (-1, -1)),
     ]
     copies = [
         pltpu.make_async_remote_copy(
@@ -96,6 +103,18 @@
         for i in group:
             copies[i].start()
 
+    def send_but_first(group):
+        for i in group:
+            dr, dc = moves[i][2]
+            to = at(dr, dc)
+            pl.when((to[0] != 0) | (to[1] != 0))(copies[i].start)
+
+    def send_first(group):
+        for i in group:
+            dr, dc = moves[i][2]
+            to = at(dr, dc)
+            pl.when((to[0] == 0) & (to[1] == 0))(copies[i].start)
+
     def arrive(group):
         for i in group:
             copies[i].wait_recv()
@@ -103,14 +122,38 @@
     def meet(dr):
         pl.semaphore_signal(met_sem, inc=1, device_id=at(dr, 1), device_id_type=MESH)
 
-    @pl.when(newest)
+    @pl.when(early)
     def _():
-        pl.semaphore_wait(barrier, 3)
-        send(EAST[:3])
-        for dr in (0, 1, -1):
-            meet(dr)
+        pl.semaphore_wait(barrier, expected)
+        send(EAST)
+
+        @pl.when(newest)
+        def _():
+            for dr in (0, 1, -1):
+                meet(dr)
+
+        @pl.when(first)
+        def _():
+            for dr, dc in ((1, 0), (-1, 0), (0, 1), (1, 1), (-1, 1)):
+                pl.semaphore_signal(first_sem, inc=1, device_id=at(dr, dc), device_id_type=MESH)
+
+    for dr in (0, 1, -1):
+        pl.when(jnp.logical_not(newest | (col == ncol - 2) | first))(functools.partial(greet, dr, 1))
+        if dr:
+            pl.when(jnp.logical_not(newest | first))(functools.partial(greet, dr, 0))
+    loads = [
+        pltpu.make_async_copy(src, dst, in_sem.at[i])
+        for i, (src, dst) in enumerate([
+            (tok.at[foot], tok_v.at[foot]), (tok.at[crown], tok_v.at[crown]), (tok.at[waist], tok_v.at[waist]),
+            (lab, lab_v), (table, tab_v), (qkv, qkv_v), (gain_one, g1_v),
+            (proj, proj_v), (gain_two, g2_v), (up, up_v), (down, down_v),
+        ])
+    ]
+    for load in loads:
+        load.start()
 
     loads[0].wait()
+    loads[1].wait()
 
     def pack(rows, high, width, packed):
         rows = rows.astype(F32)
@@ -124,20 +167,11 @@
             pieces.append(jnp.where(iota((8, width), 0) < 4, low[:, i : i + width], below))
         packed[...] = jnp.concatenate(pieces, axis=0).astype(BF16)
 
-    foot, crown = tok_v[48:64][8:16], tok_v[0:16][0:8]
-    pack(foot[:, 12 * C :], True, 256, last_east)
-    pack(crown[:, 12 * C :], False, 256, first_east)
-
-    @pl.when(newest)
-    def _():
-        send(EAST[3:])
-
-    for load in loads[1:5]:
+    pack(tok_v[48:64][8:16], True, 768, last_all)
+    pack(tok_v[0:16][0:8], False, 768, first_all)
+    pl.when(first)(functools.partial(send, ROWS))
+    for load in loads[2:7]:
         load.wait()
-    pack(foot, True, 768, last_all)
-    pack(crown, False, 768, first_all)
-    pack(foot[:, 0 : 4 * C], True, 256, last_west)
-    pack(crown[:, 0 : 4 * C], False, 256, first_west)
 
     eye = (iota((16, 64), 0) == iota((16, 64), 1)).astype(F32)
     apart = jnp.where(iota((64, 64), 0) < 16, (iota((64, 64), 0) != iota((64, 64), 1)).astype(F32) * FAR, 0.0)
@@ -185,16 +219,16 @@
     def split(wide):
         return [wide[:, C * j : C * j + C] for j in range(wide.shape[1] // C)]
 
-    def rim(above, below, base, count):
-        above, below = above.astype(F32), below.astype(F32)
-        width = above.shape[1]
-        parts = []
-        for i in range(count * C // width):
-            t = i // 2 * 8
-            over, under = above[t : t + 8], below[t : t + 8]
-            over, under = (over, pltpu.roll(under, 4, 0)) if i % 2 else (pltpu.roll(over, 4, 0), under)
-            parts.append(jnp.where(iota((8, width), 0) >= 4, over, under))
-        place(split(jnp.concatenate(parts, axis=1)), base, 64)
+    def rim(above, below):
+        return split(jnp.where(iota(above.shape, 0) >= 4, above, below))
+
+    def unpack(packed, high):
+        packed = packed.astype(F32)
+        pieces = []
+        for i in range(4):
+            piece = packed[i // 2 * 8 : i // 2 * 8 + 8]
+            pieces.append(pltpu.roll(piece, 4, 0) if (i % 2 == 1) != high else piece)
+        return jnp.concatenate(pieces, axis=1)
 
     def labels_of(above, own):
         above, own = above[...].astype(F32).T, own[...].astype(F32).T
@@ -278,7 +312,7 @@
                     row_block = piece if s == 0 else jnp.where(block32 == s, piece, row_block)
                 rows_of.append(row_block)
             turned.append(jnp.concatenate(rows_of, axis=0))
-        attended = jnp.concatenate(turned, axis=1).T.astype(BF16)
+        attended = jnp.concatenate(turned, axis=1).astype(BF16).T
         mixed = dot(attended, proj_v[...])
         for w, a in enumerate(spans[:real]):
             for x in range(nx):
@@ -301,26 +335,23 @@
         centred = residual - (mean(high) + mean(low))
         variance = mean((centred * centred).astype(BF16))
         second = (centred * lax.rsqrt(variance + 1e-05) * g2_v[...].reshape(1, C)).astype(BF16)
-        hidden = dot(second, up_v[...])
-        square = hidden * hidden
-        logit = LOGIT[6] * square + LOGIT[5]
-        for k in range(4, -1, -1):
-            logit = logit * square + LOGIT[k]
-        hidden = (hidden * (1.0 / (1.0 + jnp.exp2(hidden * logit)))).astype(BF16)
-        done = residual + lax.dot_general(hidden, down_v[...], NT, preferred_element_type=F32)
+        done = residual
+        for n in range(0, HID, 256):
+            hidden = in_pieces(32, gelu, dot(second, up_v[:, n : n + 256]))
+            done = done + lax.dot_general(hidden, down_v[:, n : n + 256], NT, preferred_element_type=F32)
         out[:, lanes] = jnp.concatenate([done[j * 64 : j * 64 + 64] for j in range(size)], axis=1).astype(BF16)
 
     place(split(tok_v[...].astype(F32)), 4, 0)
 
-    @pl.when(jnp.logical_not(newest))
+    @pl.when(jnp.logical_not(early))
     def _():
-        pl.semaphore_wait(barrier, jnp.where(oldest, 5, 8))
+        pl.semaphore_wait(barrier, expected)
+        pl.when(col == ncol - 2)(functools.partial(meet, 0))
+        send_but_first(ROWS)
         send(EAST)
-        send(ROWS)
-        pl.when(jnp.logical_not(oldest))(functools.partial(send, WEST))
-        pl.when(col == ncol - 2)(functools.partial(meet, 0))
-
-    loads[5].wait()
+        pl.when(jnp.logical_not(oldest))(functools.partial(send_but_first, WEST))
+
+    loads[7].wait()
     attend([1, 2, 3, 4, 5, 6, 7, 7], 7, 8, lambda x: 8 + x, 4, lambda: bias[...], labels_of(lab_v, lab_v), blocks64)
 
     @pl.when(newest)
@@ -329,18 +360,24 @@
         send(ROWS)
         send(WEST)
 
+    @pl.when(near_first)
+    def _():
+        pl.semaphore_wait(first_sem, 1)
+        pl.when(oldest)(functools.partial(send_first, ROWS))
+        pl.when(jnp.logical_not(oldest))(functools.partial(send_first, WEST))
+
     arrive(ROWS)
     marks = labels_of(tlab, lab_v)
     place_x = iota((72, 8), 1)
     groups[1] = marks[:, 8:16] + jnp.where((place_x >= 4) & newest, 1.0, 0.0)
-    rim(top[...], bot[...], 4, 16)
+    place(rim(unpack(top[...], True), unpack(bot[...], False)), 4, 64)
     attend([0, 8], 2, 8, lambda x: 8 + x, 4, lambda: bias[...], marks, blocks64)
-    for load in loads[6:]:
+    for load in loads[8:]:
         load.wait()
     finish(1, 8)
 
     def edge(i, carry):
-        side = jnp.where(newest, i, 1 - i)
+        side = jnp.where(oldest, 1 - i, i)
 
         @pl.when(side == 1)
         def _():
@@ -353,13 +390,16 @@
 
         @pl.when(side == 0)
         def _():
-            arrive(EAST)
+            arrive(EAST[2:4])
             near = labels_of(ltlab, llab)
             near = jnp.concatenate([near[:, 12:16], near[:, 8:12]], axis=1)
             groups[0] = near + jnp.where((place_x < 4) & oldest, 1.0, 0.0)
-
-        place(split(beside[side].astype(F32)), 20 * side, 0)
-        rim(corner[side, 0], corner[side, 1], 20 * side, 4)
+            arrive(EAST[0:2])
+            arrive(EAST[4:5])
+
+        edges = rim(corner[side, 0].astype(F32)[8:16], corner[side, 1].astype(F32)[0:8])
+        near = split(beside[side].astype(F32))
+        place([jnp.concatenate(pair, axis=0) for pair in zip(near, edges)], 20 * side, 0)
         attend(
             list(range(9)) + [8] * 3, 9, 4,
             lambda x: 16 * side + x + (1 - side) * (4 if x < 4 else -4),
@@ -378,15 +418,15 @@
     vmem = pltpu.VMEM
     scratch = [vmem(a.shape, a.dtype) for a in args]
     args = [pltpu.with_memory_space_constraint(a, pltpu.HBM) for a in args]
-    scratch += [vmem((2, 64, 768), BF16), vmem((2, 2, 16, 256), BF16)] + [vmem((16, 768), BF16)] * 2
+    scratch += [vmem((2, 64, 768), BF16), vmem((2, 2, 16, 768), BF16)] + [vmem((16, 768), BF16)] * 2
     scratch += [vmem((16, 64), jnp.int32)] * 3
-    scratch += [vmem((16, 768), BF16)] * 2 + [vmem((16, 256), BF16)] * 4
+    scratch += [vmem((16, 768), BF16)] * 2
     scratch += [vmem((24, 72, 256), F32), vmem((16, 72, C), F32), vmem((2, 72, 8), F32)]
     scratch += [vmem((C + 16, 256), BF16), vmem((C, 256), BF16), vmem((256, 256), BF16)]
     scratch += [vmem((8, 8, 128), F32), vmem((64, 384), F32), vmem((2, 64, 256), F32)]
     scratch += [vmem((10, 256, 384), BF16), vmem((12, 256, 256), BF16), vmem((12, 64, 384), F32)]
-    scratch += [pltpu.SemaphoreType.DMA((9,)), pltpu.SemaphoreType.DMA((11,)), pltpu.SemaphoreType.DMA((11,))]
-    scratch += [pltpu.SemaphoreType.REGULAR]
+    scratch += [pltpu.SemaphoreType.DMA((11,)), pltpu.SemaphoreType.DMA((11,)), pltpu.SemaphoreType.DMA((11,))]
+    scratch += [pltpu.SemaphoreType.REGULAR] * 2
     return pl.pallas_call(
         functools.partial(kernel, nrow, ncol),
         out_shape=vmem((64, 3072), BF16),

time: 23.1 us -> 22.1 us (0.957)
  Pallas kernels: 22.2 us -> 21.2 us
    pallas_call x1, Pallas kernels: 22.2 us -> 21.2 us  [local(): pl.pallas_call(functools.partial(kernel, nrow, ncol), out_shape=vmem((64,...]
where the time goes in v4:
time: 22.1 us; the launch traced here: 21.9 us
  Pallas kernels  21.2 us (96%)
  local copies, waits for them, and re-layouts  0.75 us (3%)
    pallas_call x1, Pallas kernels, local(): pl.pallas_call(functools.partial(kernel, nrow, ncol), out_shape=vmem((64,...  21.2 us
    unnamed x1, local copies, waits for them, and re-layouts  0.75 us

profile of v4, /device:TPU:1, one launch (start us, length us, event | category | flops | bytes accessed | tf_op | source)
XLA Modules:
  0.0 21.9 jit_solution(7705184225863638931)
XLA Ops:
  0.0 21.2 %window_block.1 = bf16[64,3072]{1,0:T(8,128)(2,1)S(1)} custom-call(bf16[64,3072]{1,0:T(8,128)(2,1)} %tok.1, s32[16,64]{1,0:T(8,128)} %bitcast.3, f32[192]{0:T(256)} %gain_one.1, bf16[192,576]{1,0:T(8,128)(2,1)} %qkv.1, bf16[192,192]{1,0:T(8,128)(2,1)} %proj.1, f32[6,225]{1,0:T(8,128)} %table.1, f32[192]{0:T(256)} %gain_two.1, bf16[192,768]{1,0:T(8,128)(2,1)} %up.1, ...), custom_call_target="tpu_custom_call" | custom-call | tf_op jit(solution)/shard_map/window_block/pallas_call | solution.py:430
  21.2 0.7 %copy.11 = bf16[64,3072]{1,0:T(8,128)(2,1)} copy(bf16[64,3072]{1,0:T(8,128)(2,1)S(1)} %window_block.1) | data formatting | bytes 786432

commit v5 on v4

--- a/solution.py
+++ b/solution.py
@@ -52,7 +52,7 @@
     out,
     tok_v, lab_v, g1_v, qkv_v, proj_v, tab_v, g2_v, up_v, down_v,
     beside, corner, top, bot, llab, tlab, ltlab,
-    last_all, first_all,
+    last_all, first_all, last_east, first_east, last_west, first_west,
     ext, branch, groups, wq, wv, wk, gath, bias, bias_s, blocks64, blocks32, scores_v,
     in_sem, send_sem, recv_sem, met_sem, first_sem,
 ):
@@ -78,16 +78,16 @@
     whole = pl.ds(0, 64)
     west, east = pl.ds(0, 4 * C), pl.ds(12 * C, 4 * C)
     moves = [
-        (tok.at[foot, east], corner.at[0, 0], (1, 1)),
-        (tok.at[crown, east], corner.at[0, 1], (-1, 1)),
+        (last_east, corner.at[0, 0], (1, 1)),
+        (first_east, corner.at[0, 1], (-1, 1)),
         (lab, ltlab, (1, 1)),
         (lab, llab, (0, 1)),
         (tok.at[whole, east], beside.at[0], (0, 1)),
         (last_all, top, (1, 0)),
         (first_all, bot, (-1, 0)),
         (lab, tlab, (1, 0)),
-        (tok.at[foot, west], corner.at[1, 0], (1, -1)),
-        (tok.at[crown, west], corner.at[1, 1], (-1, -1)),
+        (last_west, corner.at[1, 0], (1, -1)),
+        (first_west, corner.at[1, 1], (-1, -1)),
         (tok.at[whole, west], beside.at[1], (0, -1)),
     ]
     copies = [
@@ -122,9 +122,32 @@
     def meet(dr):
         pl.semaphore_signal(met_sem, inc=1, device_id=at(dr, 1), device_id_type=MESH)
 
+    def pack(rows, high, width, packed):
+        rows = rows.astype(F32)
+        turned = pltpu.roll(rows, 4, 0)
+        low, high = (turned, rows) if high else (rows, turned)
+        pieces = []
+        for i in range(0, rows.shape[1], 2 * width):
+            below = high[:, i + width : i + 2 * width]
+            if below.shape[1] == 0:
+                below = high[:, i : i + width]
+            pieces.append(jnp.where(iota((8, width), 0) < 4, low[:, i : i + width], below))
+        packed[...] = jnp.concatenate(pieces, axis=0).astype(BF16)
+
+    edges = [
+        pltpu.make_async_copy(tok.at[rows, east], tok_v.at[rows, east], in_sem.at[11 + i])
+        for i, rows in enumerate((foot, crown))
+    ]
+
     @pl.when(early)
     def _():
         pl.semaphore_wait(barrier, expected)
+        for edge in edges:
+            edge.start()
+        for edge in edges:
+            edge.wait()
+        pack(tok_v[48:64, 12 * C :][8:16], True, 256, last_east)
+        pack(tok_v[0:16, 12 * C :][0:8], False, 256, first_east)
         send(EAST)
 
         @pl.when(newest)
@@ -155,20 +178,16 @@
     loads[0].wait()
     loads[1].wait()
 
-    def pack(rows, high, width, packed):
-        rows = rows.astype(F32)
-        turned = pltpu.roll(rows, 4, 0)
-        low, high = (turned, rows) if high else (rows, turned)
-        pieces = []
-        for i in range(0, rows.shape[1], 2 * width):
-            below = high[:, i + width : i + 2 * width]
-            if below.shape[1] == 0:
-                below = high[:, i : i + width]
-            pieces.append(jnp.where(iota((8, width), 0) < 4, low[:, i : i + width], below))
-        packed[...] = jnp.concatenate(pieces, axis=0).astype(BF16)
-
     pack(tok_v[48:64][8:16], True, 768, last_all)
     pack(tok_v[0:16][0:8], False, 768, first_all)
+    pack(tok_v[48:64, 0 : 4 * C][8:16], True, 256, last_west)
+    pack(tok_v[0:16, 0 : 4 * C][0:8], False, 256, first_west)
+
+    @pl.when(jnp.logical_not(early))
+    def _():
+        pack(tok_v[48:64, 12 * C :][8:16], True, 256, last_east)
+        pack(tok_v[0:16, 12 * C :][0:8], False, 256, first_east)
+
     pl.when(first)(functools.partial(send, ROWS))
     for load in loads[2:7]:
         load.wait()
@@ -222,10 +241,10 @@
     def rim(above, below):
         return split(jnp.where(iota(above.shape, 0) >= 4, above, below))
 
-    def unpack(packed, high):
+    def unpack(packed, high, count=4):
         packed = packed.astype(F32)
         pieces = []
-        for i in range(4):
+        for i in range(count):
             piece = packed[i // 2 * 8 : i // 2 * 8 + 8]
             pieces.append(pltpu.roll(piece, 4, 0) if (i % 2 == 1) != high else piece)
         return jnp.concatenate(pieces, axis=1)
@@ -397,7 +416,7 @@
             arrive(EAST[0:2])
             arrive(EAST[4:5])
 
-        edges = rim(corner[side, 0].astype(F32)[8:16], corner[side, 1].astype(F32)[0:8])
+        edges = rim(unpack(corner[side, 0], True, 3), unpack(corner[side, 1], False, 3))
         near = split(beside[side].astype(F32))
         place([jnp.concatenate(pair, axis=0) for pair in zip(near, edges)], 20 * side, 0)
         attend(
@@ -418,14 +437,14 @@
     vmem = pltpu.VMEM
     scratch = [vmem(a.shape, a.dtype) for a in args]
     args = [pltpu.with_memory_space_constraint(a, pltpu.HBM) for a in args]
-    scratch += [vmem((2, 64, 768), BF16), vmem((2, 2, 16, 768), BF16)] + [vmem((16, 768), BF16)] * 2
+    scratch += [vmem((2, 64, 768), BF16), vmem((2, 2, 16, 256), BF16)] + [vmem((16, 768), BF16)] * 2
     scratch += [vmem((16, 64), jnp.int32)] * 3
-    scratch += [vmem((16, 768), BF16)] * 2
+    scratch += [vmem((16, 768), BF16)] * 2 + [vmem((16, 256), BF16)] * 4
     scratch += [vmem((24, 72, 256), F32), vmem((16, 72, C), F32), vmem((2, 72, 8), F32)]
     scratch += [vmem((C + 16, 256), BF16), vmem((C, 256), BF16), vmem((256, 256), BF16)]
     scratch += [vmem((8, 8, 128), F32), vmem((64, 384), F32), vmem((2, 64, 256), F32)]
     scratch += [vmem((10, 256, 384), BF16), vmem((12, 256, 256), BF16), vmem((12, 64, 384), F32)]
-    scratch += [pltpu.SemaphoreType.DMA((11,)), pltpu.SemaphoreType.DMA((11,)), pltpu.SemaphoreType.DMA((11,))]
+    scratch += [pltpu.SemaphoreType.DMA((13,)), pltpu.SemaphoreType.DMA((11,)), pltpu.SemaphoreType.DMA((11,))]
     scratch += [pltpu.SemaphoreType.REGULAR] * 2
     return pl.pallas_call(
         functools.partial(kernel, nrow, ncol),

time: 22.1 us -> 21.6 us (0.977)
  Pallas kernels: 21.2 us -> 20.7 us
    pallas_call x1, Pallas kernels: 21.2 us -> 20.7 us  [local(): pl.pallas_call(functools.partial(kernel, nrow, ncol), out_shape=vmem((64,...]
where the time goes in v5:
time: 21.6 us; the launch traced here: 21.4 us
  Pallas kernels  20.7 us (96%)
  local copies, waits for them, and re-layouts  0.75 us (3%)
    pallas_call x1, Pallas kernels, local(): pl.pallas_call(functools.partial(kernel, nrow, ncol), out_shape=vmem((64,...  20.7 us
    unnamed x1, local copies, waits for them, and re-layouts  0.75 us

profile of v5, /device:TPU:1, one launch (start us, length us, event | category | flops | bytes accessed | tf_op | source)
XLA Modules:
  0.0 21.4 jit_solution(13909045830608529048)
XLA Ops:
  0.0 20.7 %window_block.1 = bf16[64,3072]{1,0:T(8,128)(2,1)S(1)} custom-call(bf16[64,3072]{1,0:T(8,128)(2,1)} %tok.1, s32[16,64]{1,0:T(8,128)} %bitcast.3, f32[192]{0:T(256)} %gain_one.1, bf16[192,576]{1,0:T(8,128)(2,1)} %qkv.1, bf16[192,192]{1,0:T(8,128)(2,1)} %proj.1, f32[6,225]{1,0:T(8,128)} %table.1, f32[192]{0:T(256)} %gain_two.1, bf16[192,768]{1,0:T(8,128)(2,1)} %up.1, ...), custom_call_target="tpu_custom_call" | custom-call | tf_op jit(solution)/shard_map/window_block/pallas_call | solution.py:449
  20.7 0.7 %copy.11 = bf16[64,3072]{1,0:T(8,128)(2,1)} copy(bf16[64,3072]{1,0:T(8,128)(2,1)S(1)} %window_block.1) | data formatting | bytes 786432

commit v6 on v5

--- a/solution.py
+++ b/solution.py
@@ -54,7 +54,7 @@
     beside, corner, top, bot, llab, tlab, ltlab,
     last_all, first_all, last_east, first_east, last_west, first_west,
     ext, branch, groups, wq, wv, wk, gath, bias, bias_s, blocks64, blocks32, scores_v,
-    in_sem, send_sem, recv_sem, met_sem, first_sem,
+    in_sem, send_sem, recv_sem, met_sem, first_sem, down_t,
 ):
     row, col = lax.axis_index("row"), lax.axis_index("col")
     newest, oldest = col == ncol - 1, col == 0
@@ -357,7 +357,7 @@
         done = residual
         for n in range(0, HID, 256):
             hidden = in_pieces(32, gelu, dot(second, up_v[:, n : n + 256]))
-            done = done + lax.dot_general(hidden, down_v[:, n : n + 256], NT, preferred_element_type=F32)
+            done = done + dot(hidden, down_t[n : n + 256])
         out[:, lanes] = jnp.concatenate([done[j * 64 : j * 64 + 64] for j in range(size)], axis=1).astype(BF16)
 
     place(split(tok_v[...].astype(F32)), 4, 0)
@@ -393,6 +393,7 @@
     attend([0, 8], 2, 8, lambda x: 8 + x, 4, lambda: bias[...], marks, blocks64)
     for load in loads[8:]:
         load.wait()
+    down_t[...] = down_v[...].T
     finish(1, 8)
 
     def edge(i, carry):
@@ -445,7 +446,7 @@
     scratch += [vmem((8, 8, 128), F32), vmem((64, 384), F32), vmem((2, 64, 256), F32)]
     scratch += [vmem((10, 256, 384), BF16), vmem((12, 256, 256), BF16), vmem((12, 64, 384), F32)]
     scratch += [pltpu.SemaphoreType.DMA((13,)), pltpu.SemaphoreType.DMA((11,)), pltpu.SemaphoreType.DMA((11,))]
-    scratch += [pltpu.SemaphoreType.REGULAR] * 2
+    scratch += [pltpu.SemaphoreType.REGULAR] * 2 + [vmem((HID, C), BF16)]
     return pl.pallas_call(
         functools.partial(kernel, nrow, ncol),
         out_shape=vmem((64, 3072), BF16),

time: 21.6 us -> 21.6 us (level)
  no operation moved by 1% of the time
where the time goes in v6:
time: 21.6 us; the launch traced here: 21.5 us
  Pallas kernels  20.7 us (96%)
  local copies, waits for them, and re-layouts  0.75 us (3%)
    pallas_call x1, Pallas kernels, local(): pl.pallas_call(functools.partial(kernel, nrow, ncol), out_shape=vmem((64,...  20.7 us
    unnamed x1, local copies, waits for them, and re-layouts  0.75 us

profile of v6, /device:TPU:1, one launch (start us, length us, event | category | flops | bytes accessed | tf_op | source)
XLA Modules:
  0.0 21.5 jit_solution(15111644831578221877)
XLA Ops:
  0.0 20.7 %window_block.1 = bf16[64,3072]{1,0:T(8,128)(2,1)S(1)} custom-call(bf16[64,3072]{1,0:T(8,128)(2,1)} %tok.1, s32[16,64]{1,0:T(8,128)} %bitcast.3, f32[192]{0:T(256)} %gain_one.1, bf16[192,576]{1,0:T(8,128)(2,1)} %qkv.1, bf16[192,192]{1,0:T(8,128)(2,1)} %proj.1, f32[6,225]{1,0:T(8,128)} %table.1, f32[192]{0:T(256)} %gain_two.1, bf16[192,768]{1,0:T(8,128)(2,1)} %up.1, ...), custom_call_target="tpu_custom_call" | custom-call | tf_op jit(solution)/shard_map/window_block/pallas_call | solution.py:450
  20.7 0.7 %copy.11 = bf16[64,3072]{1,0:T(8,128)(2,1)} copy(bf16[64,3072]{1,0:T(8,128)(2,1)S(1)} %window_block.1) | data formatting | bytes 786432
